TPU v7x, 32 devices: a whole 2x2x4 slice. The times are simulated.
32 devices in a mesh: parts: 2 (over y), wide: 2 (over x), narrow: 8 (over z, core).
Axes of the slice: x: 2, y: 2, z: 4, core: 2. Of those that a mesh axis runs over, the one named last changes fastest.
Arguments:
- tokens: bfloat16 [6144, 5120], P(('parts', 'wide', 'narrow')), parts along dimension 0, may hold values from -6 to 6
- key_grad: bfloat16 [6144, 512], P(('parts', 'wide', 'narrow')), parts along dimension 0, may hold values from -12 to 12
- gain: bfloat16 [5120], replicated, may hold values from 0.099609375 to 1.8984375
- key_codes: bfloat16 [5120, 512], P('narrow'), may hold values from -4 to 4
- code_scales: bfloat16 [5120, 4], P('narrow'), may hold values from 0.0069885254 to 0.027954102
Outputs:
- token_grad: bfloat16 [6144, 5120], P(('parts', 'wide', 'narrow')), parts along dimension 0
- weight_grad: float32 [1024, 5120], P(('parts', 'wide', 'narrow')), parts along dimension 0
There are 2 independent parts, one for each index of `parts`. A program takes and returns all parts, laid end to end along the dimension named above; an argument that names none is the same for every part. Nothing has to cross between parts.
All inputs are finite; a program needn't handle non-finite values.
Results may differ from a plain program's by a relative error of at most 0.005.
Values may be sent and summed in bfloat16 or wider, within the bound.
No kernel may reach another device: no remote copies, remote signals or barrier semaphores. Data moves between devices by JAX's collectives and lax.ppermute only.
A program may use at most 64 MiB of HBM per device.

v0:
```python
import math

import jax
import jax.numpy as jnp
from jax import lax
from jax.sharding import PartitionSpec as P


def per_device(tokens, key_grad, gain, key_codes, code_scales):
    row_count = tokens.shape[0]
    feature_count = tokens.shape[1]
    key_width = key_codes.shape[1]
    group_cols = key_width // code_scales.shape[1]
    values = tokens.astype(jnp.float32)
    inverse_rms = lax.rsqrt(jnp.mean(values * values, axis=1, keepdims=True) + 1e-06)
    unit_rows = values * inverse_rms
    gain_wide = gain.astype(jnp.float32)
    normed = (unit_rows * gain_wide).astype(jnp.bfloat16)
    weight_shard = (
        key_codes.astype(jnp.float32)
        * jnp.repeat(code_scales.astype(jnp.float32), group_cols, axis=1)
    ).astype(jnp.bfloat16)
    product = lax.dot_general(
        key_grad,
        lax.all_gather(weight_shard, "narrow", axis=0, tiled=True),
        (((1,), (1,)), ((), ())),
        preferred_element_type=jnp.float32,
    )
    scaled = product * gain_wide
    inner_mean = jnp.mean(scaled * unit_rows, axis=1, keepdims=True)
    token_grad = (inverse_rms * (scaled - unit_rows * inner_mean)).astype(jnp.bfloat16)
    term = lax.dot_general(
        key_grad, normed, (((0,), (0,)), ((), ())), preferred_element_type=jnp.float32
    ).astype(jnp.bfloat16)
    wide_count = lax.axis_size("wide")
    narrow_count = lax.axis_size("narrow")
    column_block = key_width // (wide_count * narrow_count)
    blocks = term.reshape(wide_count, narrow_count, column_block, feature_count)
    received = lax.all_to_all(blocks, "narrow", split_axis=1, concat_axis=1, tiled=True)
    partial_value = jnp.sum(received.astype(jnp.float32), axis=1)
    owned = lax.all_to_all(partial_value, "wide", split_axis=0, concat_axis=0, tiled=True)
    summed = jnp.sum(owned, axis=0)
    token_total = row_count * wide_count * narrow_count
    weight_grad = summed / math.sqrt(token_total)
    return (token_grad, weight_grad)


def solution(mesh):
    return jax.shard_map(
        per_device,
        mesh=mesh,
        in_specs=(
            P(("parts", "wide", "narrow"), None),
            P(("parts", "wide", "narrow"), None),
            P(),
            P("narrow", None),
            P("narrow", None),
        ),
        out_specs=(P(("parts", "wide", "narrow"), None), P(("parts", "wide", "narrow"), None)),
        check_vma=False,
    )
```

profile of v0, /device:TPU:0, one launch (start us, length us, event | category | flops | bytes accessed | tf_op | source)
XLA Modules:
  0.0 213.6 jit_solution(12603494665329120487)
XLA Ops:
  7.2 0.0 copy-start
  7.2 0.0 copy-start.2
  7.2 0.0 copy-start.1
  7.2 0.0 all-gather.2.cloned.1.call-start
  7.2 1.0 copy.10
  8.2 0.8 broadcast_in_dim.2
  9.1 2.2 %fusion.13 = bf16[640,512]{1,0:T(8,128)(2,1)} fusion(f32[80,8,4,128]{3,2,1,0:T(4,128)S(1)} %bitcast.14, bf16[640,512]{1,0:T(8,128)(2,1)} %param.8), kind=kLoop, calls=%fused_computation.18 | loop fusion | flops 983040 | bytes 2621440 | tf_op jit(solution)/shard_map/convert_element_type | solution.py:22
  11.3 0.0 all-gather.2.cloned.1.call-update
  11.3 0.0 copy-done.2
  11.3 0.0 copy-done.1
  11.3 0.5 fusion.9
  11.8 0.0 copy-done
  11.8 1.7 convolution_convert_fusion
  13.5 2.9 %copy.11 = bf16[2,8,32,5120]{3,2,0,1:T(8,128)(2,1)} copy(bf16[2,8,32,5120]{3,2,1,0:T(8,128)(2,1)S(1)} %bitcast.13) | data formatting | bytes 10485760 | tf_op jit(solution)/shard_map/reshape | solution.py:38
  16.3 6.3 %all-to-all-start = ((bf16[2,8,32,5120]{3,2,0,1:T(8,128)(2,1)}), bf16[2,8,32,5120]{3,2,0,1:T(8,128)(2,1)}, u32[]{:S(2)}, u32[]{:S(2)}) async-start(bf16[2,8,32,5120]{3,2,0,1:T(8,128)(2,1)} %copy.11), calls=%async_computation | async-start | bytes 10485760 | tf_op jit(solution)/shard_map/all_to_all | solution.py:39
  22.6 88.8 %all-gather.2.cloned.1.call-done = bf16[5120,512]{1,0:T(8,128)(2,1)} async-done(((bf16[640,512]{1,0:T(8,128)(2,1)}), bf16[5120,512]{1,0:T(8,128)(2,1)}) %all-gather.2.cloned.1.call-update) | async-done | bytes 5242896 | tf_op jit(solution)/shard_map/all_gather | solution.py:25
  111.4 6.3 %fusion.4 = (f32[192]{0:T(256)S(1)}, f32[192,5120]{1,0:T(8,128)}) fusion(bf16[192,5120]{1,0:T(8,128)(2,1)S(1)} %copy-done.1, f32[192]{0:T(256)S(1)} %add_rsqrt_fusion, f32[5120]{0:T(1024)S(1)} %convert_element_type.34, bf16[5120,512]{1,0:T(8,128)(2,1)} %all-gather.2.cloned.1.call-done, bf16[192,512]{1,0:T(8,128)(2,1)S(1)} %copy-done), kind=kOutput, calls=%fused_computation.9 | convolution fusion | flops 1011547968 | bytes 11359744 | tf_op jit(solution)/shard_map/dot_general | solution.py:23
  117.7 62.8 %all-to-all-done = bf16[2,8,32,5120]{3,2,0,1:T(8,128)(2,1)} async-done(((bf16[2,8,32,5120]{3,2,0,1:T(8,128)(2,1)}), bf16[2,8,32,5120]{3,2,0,1:T(8,128)(2,1)}, u32[]{:S(2)}, u32[]{:S(2)}) %all-to-all-start) | async-done | bytes 5242912 | tf_op jit(solution)/shard_map/all_to_all | solution.py:39
  180.6 4.6 %convert_reduce_fusion = f32[2,32,5120]{2,1,0:T(8,128)} fusion(bf16[2,8,32,5120]{3,2,0,1:T(8,128)(2,1)} %all-to-all-done), kind=kLoop, calls=%fused_computation | loop fusion | flops 4915200 | bytes 6553600 | tf_op jit(solution)/shard_map/reduce_sum | solution.py:40
  185.2 3.6 %all-to-all-start.1 = ((f32[2,32,5120]{2,1,0:T(8,128)}), f32[2,32,5120]{2,1,0:T(8,128)S(1)}, u32[]{:S(2)}, u32[]{:S(2)}) async-start(f32[2,32,5120]{2,1,0:T(8,128)} %convert_reduce_fusion), calls=%async_computation.1 | async-start | bytes 2621440 | tf_op jit(solution)/shard_map/all_to_all | solution.py:41
  188.8 4.3 %fusion.7 = bf16[192,5120]{1,0:T(8,128)(2,1)} fusion(f32[192,5120]{1,0:T(8,128)} %get-tuple-element.3, bf16[192,5120]{1,0:T(8,128)(2,1)S(1)} %copy-done.1, f32[192]{0:T(256)S(1)} %broadcast_multiply_fusion.1, f32[192]{0:T(256)S(1)} %add_rsqrt_fusion), kind=kLoop, calls=%fused_computation.12 | loop fusion | flops 5898240 | bytes 7865856 | tf_op jit(solution)/shard_map/convert_element_type | solution.py:31
  193.1 12.6 %all-to-all-done.1 = f32[2,32,5120]{2,1,0:T(8,128)S(1)} async-done(((f32[2,32,5120]{2,1,0:T(8,128)}), f32[2,32,5120]{2,1,0:T(8,128)S(1)}, u32[]{:S(2)}, u32[]{:S(2)}) %all-to-all-start.1) | async-done | bytes 1310752 | tf_op jit(solution)/shard_map/all_to_all | solution.py:41
  205.7 0.1 reduce_sum.39
  205.9 0.9 broadcast_multiply_fusion
  (3 shorter events, 0.0 us)
Async XLA Ops:
  7.2 4.6 %copy-start = (bf16[192,512]{1,0:T(8,128)(2,1)S(1)}, bf16[192,512]{1,0:T(8,128)(2,1)}, u32[]{:S(2)}) copy-start(bf16[192,512]{1,0:T(8,128)(2,1)} %param.6) | copy-start | bytes 589828
  7.2 4.1 %copy-start.2 = (bf16[5120]{0:T(1024)(128)(2,1)S(1)}, bf16[5120]{0:T(1024)(128)(2,1)}, u32[]{:S(2)}) copy-start(bf16[5120]{0:T(1024)(128)(2,1)} %param.7) | copy-start | bytes 30724
  7.2 4.1 %copy-start.1 = (bf16[192,5120]{1,0:T(8,128)(2,1)S(1)}, bf16[192,5120]{1,0:T(8,128)(2,1)}, u32[]{:S(2)}) copy-start(bf16[192,5120]{1,0:T(8,128)(2,1)} %param.5) | copy-start | bytes 5898244
  7.2 104.2 %all-gather.2.cloned.1.call-start = ((), (), s32[]{:S(2)}) async-start(), calls=%async_computation.2 | async-start | bytes 5898240 | tf_op jit(solution)/shard_map/all_gather | solution.py:25
  16.3 164.3 %all-to-all-start = ((bf16[2,8,32,5120]{3,2,0,1:T(8,128)(2,1)}), bf16[2,8,32,5120]{3,2,0,1:T(8,128)(2,1)}, u32[]{:S(2)}, u32[]{:S(2)}) async-start(bf16[2,8,32,5120]{3,2,0,1:T(8,128)(2,1)} %copy.11), calls=%async_computation | async-start | bytes 10485760 | tf_op jit(solution)/shard_map/all_to_all | solution.py:39
  185.2 20.6 %all-to-all-start.1 = ((f32[2,32,5120]{2,1,0:T(8,128)}), f32[2,32,5120]{2,1,0:T(8,128)S(1)}, u32[]{:S(2)}, u32[]{:S(2)}) async-start(f32[2,32,5120]{2,1,0:T(8,128)} %convert_reduce_fusion), calls=%async_computation.1 | async-start | bytes 2621440 | tf_op jit(solution)/shard_map/all_to_all | solution.py:41
Sparse Core Ops, SparseCore 0:
  11.4 99.9 all-gather.1
where the time goes:
time: 214 us
  waiting for transfers between devices  164 us (77%)
  between operations  14.1 us (7%)
  other arithmetic  12.6 us (6%)
  starting transfers between devices  9.99 us (5%)
  matrix products  7.95 us (4%)
  local copies, waits for them, and re-layouts  4.69 us (2%)
    all_gather x1, waiting for transfers between devices, per_device(): lax.all_gather(weight_shard, 'narrow', axis=0, tiled=True)  88.8 us
    all_to_all x1, waiting for transfers between devices, per_device(): lax.all_to_all(blocks, 'narrow', split_axis=1, concat_axis=1, tiled=True)  62.8 us
    all_to_all x1, waiting for transfers between devices, per_device(): lax.all_to_all(partial_value, 'wide', split_axis=0, concat_axis=0, tiled=...  12.6 us
    all_to_all x1, starting transfers between devices, per_device(): lax.all_to_all(blocks, 'narrow', split_axis=1, concat_axis=1, tiled=True)  6.32 us
    dot_general x1, matrix products, per_device(): lax.dot_general(key_grad, lax.all_gather(weight_shard, 'narrow', axis=0,...  6.3 us
    reduce_sum x1, other arithmetic, per_device(): partial_value = jnp.sum(received.astype(jnp.float32), axis=1)  4.59 us
    convert_element_type x1, other arithmetic, per_device(): (inverse_rms * (scaled - unit_rows * inner_mean)).astype(jnp.bfloat16)  4.32 us
  transfers between devices with their start and end apart: 3, of which 3 were waited for; matrix products, arithmetic and copies ran while one was open for 7% of the time, Pallas kernels for 0%

commit v1 on v0

v1 whole, which is shorter than its diff:
```python
import functools
import math

import jax
import jax.numpy as jnp
from jax import lax
from jax.experimental import pallas as pl
from jax.experimental.pallas import tpu as pltpu
from jax.sharding import PartitionSpec as P

F32, BF16 = jnp.float32, jnp.bfloat16
EPS = 1e-06
ROWS = 16
NT = (((1,), (1,)), ((), ()))


def general(tokens, key_grad, gain, key_codes, code_scales):
    row_count = tokens.shape[0]
    feature_count = tokens.shape[1]
    key_width = key_codes.shape[1]
    group_cols = key_width // code_scales.shape[1]
    values = tokens.astype(F32)
    inverse_rms = lax.rsqrt(jnp.mean(values * values, axis=1, keepdims=True) + EPS)
    unit_rows = values * inverse_rms
    gain_wide = gain.astype(F32)
    normed = (unit_rows * gain_wide).astype(BF16)
    weight_shard = (
        key_codes.astype(F32) * jnp.repeat(code_scales.astype(F32), group_cols, axis=1)
    ).astype(BF16)
    product = lax.dot_general(
        key_grad,
        lax.all_gather(weight_shard, "narrow", axis=0, tiled=True),
        NT,
        preferred_element_type=F32,
    )
    scaled = product * gain_wide
    inner_mean = jnp.mean(scaled * unit_rows, axis=1, keepdims=True)
    token_grad = (inverse_rms * (scaled - unit_rows * inner_mean)).astype(BF16)
    term = lax.dot_general(
        key_grad, normed, (((0,), (0,)), ((), ())), preferred_element_type=F32
    ).astype(BF16)
    wide_count = lax.axis_size("wide")
    narrow_count = lax.axis_size("narrow")
    column_block = key_width // (wide_count * narrow_count)
    blocks = term.reshape(wide_count, narrow_count, column_block, feature_count)
    received = lax.all_to_all(blocks, "narrow", split_axis=1, concat_axis=1, tiled=True)
    partial_value = jnp.sum(received.astype(F32), axis=1)
    owned = lax.all_to_all(partial_value, "wide", split_axis=0, concat_axis=0, tiled=True)
    summed = jnp.sum(owned, axis=0)
    token_total = row_count * wide_count * narrow_count
    weight_grad = summed / math.sqrt(token_total)
    return (token_grad, weight_grad)


def call(kernel, out_shape, scratch=(), n_in=1, flops=0, nbytes=0, limit=48, name=None):
    vmem = pl.BlockSpec(memory_space=pltpu.VMEM)
    return pl.pallas_call(
        kernel,
        out_shape=out_shape,
        in_specs=[vmem] * n_in,
        out_specs=jax.tree.map(lambda _: vmem, out_shape),
        scratch_shapes=list(scratch),
        compiler_params=pltpu.CompilerParams(vmem_limit_bytes=limit * 2**20),
        cost_estimate=pl.CostEstimate(flops=flops, bytes_accessed=nbytes, transcendentals=0),
        name=name,
    )


def inverse_rms_into(tok_ref, inv_ref, lanes=1280):
    rows, width = tok_ref.shape

    def step(i, carry):
        at = pl.multiple_of(i * ROWS, ROWS)
        total = jnp.zeros((ROWS, 128), F32)
        for j in range(width // lanes):
            v = tok_ref[pl.ds(at, ROWS), j * lanes : (j + 1) * lanes].astype(F32)
            v = v * v
            for k in range(lanes // 128):
                total = total + v[:, k * 128 : (k + 1) * 128]
        mean = jnp.sum(total, axis=1, keepdims=True) * (1.0 / width)
        inv_ref[pl.ds(at, ROWS), :] = jnp.broadcast_to(lax.rsqrt(mean + EPS), (ROWS, 128))
        return carry

    lax.fori_loop(0, rows // ROWS, step, 0)


def decode_kernel(tok_ref, code_ref, scale_ref, inv_ref, sent_ref, kept_ref):
    groups = scale_ref.shape[1]
    cols = code_ref.shape[1] // groups
    side = lax.axis_index("parts")
    half = groups // 2
    scales = scale_ref[...].astype(F32)
    for g in range(groups):
        block = (code_ref[:, g * cols : (g + 1) * cols].astype(F32) * scales[:, g : g + 1]).astype(BF16)
        at = (g % half) * cols

        @pl.when(side == g // half)
        def _():
            sent_ref[:, at : at + cols] = block

        @pl.when(side != g // half)
        def _():
            kept_ref[:, at : at + cols] = block

    inverse_rms_into(tok_ref, inv_ref)


def term_kernel(first, count, tok_a, tok_b, inv_a, kg_a, kg_b, gain_ref, *refs):
    if first == 0:
        sent_ref, kept_ref, inv_b, select_ref, normed, picked = refs
    else:
        inv_b, select_ref, sent_ref, kept_ref, normed = refs
        picked = select_ref
    rows = tok_a.shape[0]
    if first == 0:
        inverse_rms_into(tok_b, inv_b)
        keys = kg_a.shape[1]
        wide, spot = lax.axis_index("wide"), lax.axis_index("narrow")
        z, core = spot // 2, spot % 2
        row = lax.broadcasted_iota(jnp.int32, (256, keys), 0)
        col = lax.broadcasted_iota(jnp.int32, (256, keys), 1)
        group = row // 32
        order = group % 4
        apart = (order % 2) * 2 + order // 2
        target = 256 * jnp.where(group < 4, 1 - wide, wide) + 64 * (apart ^ z) + 32 * core + row % 32
        pick = jnp.where(col == target, 1.0, 0.0).astype(BF16)
        for n, kg in enumerate((kg_a, kg_b)):
            picked[:, n * rows : (n + 1) * rows] = lax.dot_general(
                pick, kg[...], NT, preferred_element_type=F32
            ).astype(BF16)
        select_ref[...] = picked[...]
    gain = gain_ref[:, first : first + count].astype(F32)
    for n, (tok, inv) in enumerate(((tok_a, inv_a), (tok_b, inv_b))):

        def step(i, carry):
            at = pl.multiple_of(i * ROWS, ROWS)
            scale = inv[pl.ds(at, ROWS), :]
            for j in range(0, count, 128):
                v = tok[pl.ds(at, ROWS), first + j : first + j + 128].astype(F32)
                normed[pl.ds(n * rows + at, ROWS), j : j + 128] = (v * scale * gain[:, j : j + 128]).astype(BF16)
            return carry

        lax.fori_loop(0, rows // ROWS, step, 0)
    tile = 512 if count % 512 == 0 else 256
    for j in range(0, count, tile):
        term = jnp.dot(picked[...], normed[:, j : j + tile], preferred_element_type=F32).astype(BF16)
        sent_ref[:, j : j + tile] = term[:128]
        kept_ref[:, j : j + tile] = term[128:]


def product_kernel(blocks, kg_a, kg_b, *refs):
    parts, (own_ref, sent_ref) = refs[: 2 * blocks], refs[2 * blocks :]
    side = lax.axis_index("parts")
    half = kg_a.shape[1] // 2
    near = pl.ds(pl.multiple_of(side * half, half), half)
    far = pl.ds(pl.multiple_of((1 - side) * half, half), half)
    width = parts[0].shape[0]
    for kg, out in ((kg_b, sent_ref), (kg_a, own_ref)):
        a, b = kg[:, near], kg[:, far]
        for n in range(blocks):
            value = lax.dot_general(a, parts[2 * n][...], NT, preferred_element_type=F32)
            value = value + lax.dot_general(b, parts[2 * n + 1][...], NT, preferred_element_type=F32)
            out[:, n * width : (n + 1) * width] = value.astype(out.dtype)


def token_kernel(counts, tok_ref, inv_ref, gain_ref, *refs):
    pieces, (out_ref, scaled_ref) = refs[:-2], refs[-2:]
    rows, width = tok_ref.shape
    spot = lax.axis_index("narrow")
    z, core = spot // 2, spot % 2
    block = width // 8
    table = []
    k = 0
    for p, count in enumerate(counts):
        for n in range(count):
            for m in range(2):
                who = core if m == 0 else 1 - core
                at = pl.multiple_of(block * (2 * (z ^ k) + who), 128)
                table.append((pieces[2 * p + m], n * block, at, (2 * k + m) * block))
            k += 1

    def step(i, carry):
        r = pl.ds(pl.multiple_of(i * ROWS, ROWS), ROWS)
        inv = inv_ref[r, :]
        total = jnp.zeros((ROWS, 128), F32)
        for ref, start, at, keep in table:
            for j in range(0, block, 128):
                scaled = ref[r, start + j : start + j + 128].astype(F32) * gain_ref[:, pl.ds(at + j, 128)].astype(F32)
                scaled_ref[:, keep + j : keep + j + 128] = scaled
                total = total + scaled * (tok_ref[r, pl.ds(at + j, 128)].astype(F32) * inv)
        mean = jnp.sum(total, axis=1, keepdims=True) * (1.0 / width)
        for ref, start, at, keep in table:
            for j in range(0, block, 128):
                unit = tok_ref[r, pl.ds(at + j, 128)].astype(F32) * inv
                out_ref[r, pl.ds(at + j, 128)] = (inv * (scaled_ref[:, keep + j : keep + j + 128] - unit * mean)).astype(BF16)
        return carry

    lax.fori_loop(0, rows // ROWS, step, 0)


def swap_pairs(count, bit):
    return [(i, i ^ bit) for i in range(count)]


def tuned(tokens, key_grad, gain, key_codes, code_scales):
    rows, width = tokens.shape
    keys = key_grad.shape[1]
    S = jax.ShapeDtypeStruct
    swap = lambda a, axis, bit: lax.ppermute(a, axis, swap_pairs(lax.axis_size(axis), bit))
    core = lambda a: swap(a, "narrow", 1)
    near = lambda a: swap(a, "narrow", 2)
    far = lambda a: swap(a, "narrow", 4)
    across = lambda a: swap(a, "wide", 1)
    beside = lambda a: swap(a, "parts", 1)
    gain_row = gain.reshape(1, width)
    shard = key_codes.shape[0]

    tok_b, kg_b = core(tokens), core(key_grad)
    inv_a, unit, rest = call(
        decode_kernel,
        (S((rows, 128), F32), S((shard, keys // 2), BF16), S((shard, keys // 2), BF16)),
        n_in=3, nbytes=4 * 2**20, name="decode",
    )(tokens, key_codes, code_scales)
    unit_1 = near(unit)
    unit_2 = far(unit)

    cut = width // 2
    half = (S((128, cut), BF16),) * 2
    sent_0, kept_0, inv_b, picked = call(
        functools.partial(term_kernel, 0, cut),
        half + (S((rows, 128), F32), S((256, 2 * rows), BF16)),
        scratch=(pltpu.VMEM((2 * rows, cut), BF16), pltpu.VMEM((256, 2 * rows), BF16)),
        n_in=6, flops=2 * 256 * 2 * rows * cut, nbytes=6 * 2**20, name="term_first",
    )(tokens, tok_b, inv_a, key_grad, kg_b, gain_row)
    sent_1, kept_1 = call(
        functools.partial(term_kernel, cut, cut),
        half,
        scratch=(pltpu.VMEM((2 * rows, cut), BF16),),
        n_in=8, flops=2 * 256 * 2 * rows * cut, nbytes=6 * 2**20, name="term_second",
    )(tokens, tok_b, inv_a, key_grad, kg_b, gain_row, inv_b, picked)

    got_0, got_1 = across(sent_0), across(sent_1)
    unit_3 = near(unit_2)
    other_1, other_2, other_3 = beside(unit_1), beside(unit_2), beside(unit_3)

    owned = []
    for kept, got in ((kept_0, got_0), (kept_1, got_1)):
        total = kept.astype(F32) + got.astype(F32)
        got = near(total[64:].astype(BF16))
        total = total[:64] + got.astype(F32)
        got = far(total[32:].astype(BF16))
        owned.append(total[:32] + got.astype(F32))
    weight_grad = jnp.concatenate(owned, axis=1) / math.sqrt(rows * lax.axis_size("wide") * lax.axis_size("narrow"))

    def product(*parts):
        n = len(parts) // 2
        own, sent = call(
            functools.partial(product_kernel, n),
            (S((rows, n * shard), F32), S((rows, n * shard), BF16)),
            n_in=2 + 2 * n, flops=2 * 2 * rows * keys * n * shard, nbytes=4 * 2**20, name="product",
        )(key_grad, kg_b, *parts)
        return own, core(sent)

    most = product(unit, rest, unit_1, other_1, unit_2, other_2)
    last = product(unit_3, other_3)
    token_grad = call(
        functools.partial(token_kernel, (3, 1)),
        S((rows, width), BF16),
        scratch=(pltpu.VMEM((ROWS, width), F32),),
        n_in=7, nbytes=8 * 2**20, name="token_grad",
    )(tokens, inv_a, gain_row, *most, *last)
    return (token_grad, weight_grad)


def solution(mesh):
    sizes = dict(mesh.shape)
    fits = sizes["parts"] == 2 and sizes["wide"] == 2 and sizes["narrow"] == 8
    return jax.shard_map(
        tuned if fits else general,
        mesh=mesh,
        in_specs=(
            P(("parts", "wide", "narrow"), None),
            P(("parts", "wide", "narrow"), None),
            P(),
            P("narrow", None),
            P("narrow", None),
        ),
        out_specs=(P(("parts", "wide", "narrow"), None), P(("parts", "wide", "narrow"), None)),
        check_vma=False,
    )
```

time: 214 us -> 106 us (0.50)
  waiting for transfers between devices: 164 us -> 66.9 us
  between operations: 14.1 us -> 0.79 us
  Pallas kernels: 0 us -> 12.9 us
  other arithmetic: 12.6 us -> 1.4 us
  starting transfers between devices: 9.99 us -> 20.1 us
  matrix products: 7.95 us -> 0 us
    all_gather x1 -> x0, waiting for transfers between devices: 88.8 us -> none  [per_device(): lax.all_gather(weight_shard, 'narrow', axis=0, tiled=True)]
    all_to_all x2 -> x0, waiting for transfers between devices: 75.5 us -> none  [the longest x1 62.8 us: per_device(): lax.all_to_all(blocks, 'narrow', split_axis=1, concat_axis=1, tiled=True)]
    ppermute x0 -> x16, waiting for transfers between devices: none -> 66.9 us  [tuned(): lax.ppermute(a, axis, swap_pairs(lax.axis_size(axis), bit))]
    ppermute x0 -> x16, starting transfers between devices: none -> 20.1 us  [tuned(): lax.ppermute(a, axis, swap_pairs(lax.axis_size(axis), bit))]
    pallas_call x0 -> x6, Pallas kernels: none -> 12.9 us  [the longest x1 3.88 us: tuned(): call(functools.partial(token_kernel, (3, 1)), S((rows, width), BF16), scr...]
    all_to_all x2 -> x0, starting transfers between devices: 9.95 us -> none  [the longest x1 6.32 us: per_device(): lax.all_to_all(blocks, 'narrow', split_axis=1, concat_axis=1, tiled=True)]
    dot_general x2 -> x0, matrix products: 7.95 us -> none  [the longest x1 6.3 us: per_device(): lax.dot_general(key_grad, lax.all_gather(weight_shard, 'narrow', axis=0,...]
    convert_element_type x3 -> x0, other arithmetic: 6.5 us -> none  [the longest x1 4.32 us: per_device(): (inverse_rms * (scaled - unit_rows * inner_mean)).astype(jnp.bfloat16)]
  transfers between devices with their start and end apart: 3 -> 16, of which waited for: 3 -> 9; matrix products, arithmetic and copies ran while one was open for 7% -> 1% of each run, Pallas kernels for 0% -> 12%
where the time goes in v1:
time: 106 us
  waiting for transfers between devices  66.9 us (63%)
  starting transfers between devices  20.1 us (19%)
  Pallas kernels  12.9 us (12%)
  local copies, waits for them, and re-layouts  3.66 us (3%)
  other arithmetic  1.4 us (1%)
    ppermute x16, waiting for transfers between devices, tuned(): lax.ppermute(a, axis, swap_pairs(lax.axis_size(axis), bit))  66.9 us
    ppermute x16, starting transfers between devices, tuned(): lax.ppermute(a, axis, swap_pairs(lax.axis_size(axis), bit))  20.1 us
    pallas_call x1, Pallas kernels, tuned(): call(functools.partial(token_kernel, (3, 1)), S((rows, width), BF16), scr...  3.88 us
    unnamed x11, local copies, waits for them, and re-layouts  3.54 us
    pallas_call x1, Pallas kernels, tuned(): call(functools.partial(term_kernel, 0, cut), half + (S((rows, 128), F32),...  3.49 us
  transfers between devices with their start and end apart: 16, of which 9 were waited for; matrix products, arithmetic and copies ran while one was open for 1% of the time, Pallas kernels for 12%

profile of v1, /device:TPU:0, one launch (start us, length us, event | category | flops | bytes accessed | tf_op | source)
XLA Modules:
  0.0 105.8 jit_solution(15616298183502275277)
XLA Ops:
  0.6 0.5 collective-permute-start.9
  1.1 0.9 copy.7.scale_ref
  2.0 1.5 %copy-done = bf16[192,5120]{1,0:T(8,128)(2,1)S(1)} copy-done((bf16[192,5120]{1,0:T(8,128)(2,1)S(1)}, bf16[192,5120]{1,0:T(8,128)(2,1)}, u32[]{:S(2)}) %copy-start) | copy-done | bytes 1966104
  3.6 1.1 %copy-done.3 = bf16[640,512]{1,0:T(8,128)(2,1)S(1)} copy-done((bf16[640,512]{1,0:T(8,128)(2,1)S(1)}, bf16[640,512]{1,0:T(8,128)(2,1)}, u32[]{:S(2)}) %copy-start.3) | copy-done | bytes 655384
  4.7 2.1 %decode.1 = (f32[192,128]{1,0:T(8,128)S(1)}, bf16[640,256]{1,0:T(8,128)(2,1)S(1)}, bf16[640,256]{1,0:T(8,128)(2,1)S(1)}) custom-call(bf16[192,5120]{1,0:T(8,128)(2,1)S(1)} %copy-done, bf16[640,512]{1,0:T(8,128)(2,1)S(1)} %copy-done.3, bf16[640,4]{1,0:T(8,128)(2,1)S(1)} %copy.7.scale_ref), custom_call_target="tpu_custom_call" | custom-call | bytes 4194304 | tf_op jit(solution)/shard_map/decode/pallas_call | solution.py:219
  6.7 3.6 %collective-permute-start.3 = (bf16[640,256]{1,0:T(8,128)(2,1)S(1)}, bf16[640,256]{1,0:T(8,128)(2,1)S(1)}, u32[]{:S(2)}, u32[]{:S(2)}) collective-permute-start(bf16[640,256]{1,0:T(8,128)(2,1)S(1)} %get-tuple-element.16.refs_0_), channel_id=1, source_target_pairs={{0,4},{1,5},{2,6},{3,7},{4,0},{5,1},{6,2},{7,3},{8,12},{9,13},{10,... | collective-permute-start | bytes 983048 | tf_op jit(solution)/shard_map/ppermute | solution.py:209
  10.4 1.6 %collective-permute-start.1 = (bf16[640,256]{1,0:T(8,128)(2,1)S(1)}, bf16[640,256]{1,0:T(8,128)(2,1)S(1)}, u32[]{:S(2)}, u32[]{:S(2)}) collective-permute-start(bf16[640,256]{1,0:T(8,128)(2,1)S(1)} %get-tuple-element.16.refs_0_), channel_id=1, source_target_pairs={{0,2},{1,3},{2,0},{3,1},{4,6},{5,7},{6,4},{7,5},{8,10},{9,11},{10,... | collective-permute-start | bytes 983048 | tf_op jit(solution)/shard_map/ppermute | solution.py:209
  11.9 13.9 %collective-permute-done.3.refs_4_ = bf16[640,256]{1,0:T(8,128)(2,1)S(1)} collective-permute-done((bf16[640,256]{1,0:T(8,128)(2,1)S(1)}, bf16[640,256]{1,0:T(8,128)(2,1)S(1)}, u32[]{:S(2)}, u32[]{:S(2)}) %collective-permute-start.3) | collective-permute-done | bytes 327712 | tf_op jit(solution)/shard_map/ppermute | solution.py:209
  25.9 1.6 %collective-permute-start.4 = (bf16[640,256]{1,0:T(8,128)(2,1)S(1)}, bf16[640,256]{1,0:T(8,128)(2,1)S(1)}, u32[]{:S(2)}, u32[]{:S(2)}) collective-permute-start(bf16[640,256]{1,0:T(8,128)(2,1)S(1)} %collective-permute-done.3.refs_4_), channel_id=1, source_target_pairs={{0,16},{16,0},{1,17},{17,1},{2,18},{18,2},{3,19},{19,3},{4,20},{20... | collective-permute-start | bytes 983048 | tf_op jit(solution)/shard_map/ppermute | solution.py:209
  27.4 0.5 collective-permute-start.2
  27.9 1.2 %collective-permute-start.6 = (bf16[640,256]{1,0:T(8,128)(2,1)S(1)}, bf16[640,256]{1,0:T(8,128)(2,1)S(1)}, u32[]{:S(2)}, u32[]{:S(2)}) collective-permute-start(bf16[640,256]{1,0:T(8,128)(2,1)S(1)} %collective-permute-done.3.refs_4_), channel_id=1, source_target_pairs={{0,2},{1,3},{2,0},{3,1},{4,6},{5,7},{6,4},{7,5},{8,10},{9,11},{10,... | collective-permute-start | bytes 983048 | tf_op jit(solution)/shard_map/ppermute | solution.py:209
  29.1 0.3 collective-permute-done.kg_b
  29.3 7.1 %collective-permute-done.4.refs_5_ = bf16[640,256]{1,0:T(8,128)(2,1)S(1)} collective-permute-done((bf16[640,256]{1,0:T(8,128)(2,1)S(1)}, bf16[640,256]{1,0:T(8,128)(2,1)S(1)}, u32[]{:S(2)}, u32[]{:S(2)}) %collective-permute-start.4) | collective-permute-done | bytes 327712 | tf_op jit(solution)/shard_map/ppermute | solution.py:209
  36.4 5.9 %collective-permute-done.2.refs_3_ = bf16[640,256]{1,0:T(8,128)(2,1)S(1)} collective-permute-done((bf16[640,256]{1,0:T(8,128)(2,1)S(1)}, bf16[640,256]{1,0:T(8,128)(2,1)S(1)}, u32[]{:S(2)}, u32[]{:S(2)}) %collective-permute-start.2) | collective-permute-done | bytes 327712 | tf_op jit(solution)/shard_map/ppermute | solution.py:209
  42.4 1.4 %product.2 = (f32[192,1920]{1,0:T(8,128)S(1)}, bf16[192,1920]{1,0:T(8,128)(2,1)S(1)}) custom-call(bf16[192,512]{1,0:T(8,128)(2,1)S(1)} %copy-done.2, bf16[192,512]{1,0:T(8,128)(2,1)S(1)} %collective-permute-done.kg_b, bf16[640,256]{1,0:T(8,128)(2,1)S(1)} %get-tuple-element.16.refs_0_, bf16[640,256]{1,0:T(8,128)(2,1)S(1)} %get-tuple-element.17.refs_1_, ...), custom_call_target="tpu_custom_call" | custom-call | flops 754974720 | bytes 4194304 | tf_op jit(solution)/shard_map/product/pallas_call | solution.py:257
  43.9 3.5 %term_first.1 = (bf16[128,2560]{1,0:T(8,128)(2,1)S(1)}, bf16[128,2560]{1,0:T(8,128)(2,1)S(1)}, f32[192,128]{1,0:T(8,128)S(1)}, bf16[256,384]{1,0:T(8,128)(2,1)S(1)}) custom-call(bf16[192,5120]{1,0:T(8,128)(2,1)S(1)} %copy-done.1, bf16[192,5120]{1,0:T(8,128)(2,1)S(1)} %collective-permute-done.9.tok_b, f32[192,128]{1,0:T(8,128)S(1)} %get-tuple-element.15.inv_ref.inv_a, ...), custom_call_target="tpu_custom_call" | custom-call | flops 503316480 | bytes 6291456 | tf_op jit(solution)/shard_map/term_first/pallas_call | solution.py:229
  47.4 1.4 %collective-permute-start.10 = (bf16[128,2560]{1,0:T(8,128)(2,1)S(1)}, bf16[128,2560]{1,0:T(8,128)(2,1)S(1)}, u32[]{:S(2)}, u32[]{:S(2)}) collective-permute-start(bf16[128,2560]{1,0:T(8,128)(2,1)S(1)} %get-tuple-element.23), channel_id=1, source_target_pairs={{0,8},{8,0},{1,9},{9,1},{2,10},{10,2},{3,11},{11,3},{4,12},{12,4},... | collective-permute-start | bytes 1966088 | tf_op jit(solution)/shard_map/ppermute | solution.py:209
  48.8 1.5 %collective-permute-start.7 = (bf16[640,256]{1,0:T(8,128)(2,1)S(1)}, bf16[640,256]{1,0:T(8,128)(2,1)S(1)}, u32[]{:S(2)}, u32[]{:S(2)}) collective-permute-start(bf16[640,256]{1,0:T(8,128)(2,1)S(1)} %collective-permute-done.6.refs_0_), channel_id=1, source_target_pairs={{0,16},{16,0},{1,17},{17,1},{2,18},{18,2},{3,19},{19,3},{4,20},{20... | collective-permute-start | bytes 983048 | tf_op jit(solution)/shard_map/ppermute | solution.py:209
  50.3 8.3 %collective-permute-done.7.refs_1_ = bf16[640,256]{1,0:T(8,128)(2,1)S(1)} collective-permute-done((bf16[640,256]{1,0:T(8,128)(2,1)S(1)}, bf16[640,256]{1,0:T(8,128)(2,1)S(1)}, u32[]{:S(2)}, u32[]{:S(2)}) %collective-permute-start.7) | collective-permute-done | bytes 327712 | tf_op jit(solution)/shard_map/ppermute | solution.py:209
  58.6 0.6 product.3
  59.3 1.5 %collective-permute-done.8.refs_3_ = bf16[192,640]{1,0:T(8,128)(2,1)S(1)} collective-permute-done((bf16[192,640]{1,0:T(8,128)(2,1)S(1)}, bf16[192,640]{1,0:T(8,128)(2,1)S(1)}, u32[]{:S(2)}, u32[]{:S(2)}) %collective-permute-start.8) | collective-permute-done | bytes 245792 | tf_op jit(solution)/shard_map/ppermute | solution.py:209
  60.8 3.9 %token_grad.1 = bf16[192,5120]{1,0:T(8,128)(2,1)} custom-call(bf16[192,5120]{1,0:T(8,128)(2,1)S(1)} %copy-done.1, f32[192,128]{1,0:T(8,128)S(1)} %get-tuple-element.15.inv_ref.inv_a, bf16[1,5120]{1,0:T(2,128)(2,1)S(1)} %reshape.7.gain_ref, f32[192,1920]{1,0:T(8,128)S(1)} %get-tuple-element.18.refs_0_, bf16[192,1920]{1,0:T(8,128)(2,1)S(1)} %collective-permute-done.5.refs_1_, ...), custom_call_target="tpu_custom_call" | custom-call | bytes 8388608 | tf_op jit(solution)/shard_map/token_grad/pallas_call | solution.py:266
  64.7 1.5 %term_second.1 = (bf16[128,2560]{1,0:T(8,128)(2,1)S(1)}, bf16[128,2560]{1,0:T(8,128)(2,1)S(1)}) custom-call(bf16[192,5120]{1,0:T(8,128)(2,1)S(1)} %copy-done.1, bf16[192,5120]{1,0:T(8,128)(2,1)S(1)} %collective-permute-done.9.tok_b, f32[192,128]{1,0:T(8,128)S(1)} %get-tuple-element.15.inv_ref.inv_a, bf16[192,512]{1,0:T(8,128)(2,1)S(1)} %copy-done.2, ...), custom_call_target="tpu_custom_call" | custom-call | flops 503316480 | bytes 6291456 | tf_op jit(solution)/shard_map/term_second/pallas_call | solution.py:235
  66.2 0.8 collective-permute-start.13
  67.1 0.9 collective-permute-start.11
  68.1 15.0 %collective-permute-done.13 = bf16[128,2560]{1,0:T(8,128)(2,1)S(1)} collective-permute-done((bf16[128,2560]{1,0:T(8,128)(2,1)S(1)}, bf16[128,2560]{1,0:T(8,128)(2,1)S(1)}, u32[]{:S(2)}, u32[]{:S(2)}) %collective-permute-start.13) | collective-permute-done | bytes 655392 | tf_op jit(solution)/shard_map/ppermute | solution.py:209
  83.2 1.1 collective-permute-start.14
  84.4 3.4 %collective-permute-start.12 = (bf16[32,2560]{1,0:T(8,128)(2,1)S(1)}, bf16[32,2560]{1,0:T(8,128)(2,1)S(1)}, u32[]{:S(2)}, u32[]{:S(2)}) collective-permute-start(bf16[32,2560]{1,0:T(8,128)(2,1)S(1)} %slice.55), channel_id=1, source_target_pairs={{0,4},{1,5},{2,6},{3,7},{4,0},{5,1},{6,2},{7,3},{8,12},{9,13},{10,... | collective-permute-start | bytes 491528 | tf_op jit(solution)/shard_map/ppermute | solution.py:209
  87.8 7.9 %collective-permute-done.14 = bf16[64,2560]{1,0:T(8,128)(2,1)S(1)} collective-permute-done((bf16[64,2560]{1,0:T(8,128)(2,1)S(1)}, bf16[64,2560]{1,0:T(8,128)(2,1)S(1)}, u32[]{:S(2)}, u32[]{:S(2)}) %collective-permute-start.14) | collective-permute-done | bytes 327712 | tf_op jit(solution)/shard_map/ppermute | solution.py:209
  95.8 1.9 %collective-permute-start.15 = (bf16[32,2560]{1,0:T(8,128)(2,1)S(1)}, bf16[32,2560]{1,0:T(8,128)(2,1)S(1)}, u32[]{:S(2)}, u32[]{:S(2)}) collective-permute-start(bf16[32,2560]{1,0:T(8,128)(2,1)S(1)} %slice.54), channel_id=1, source_target_pairs={{0,4},{1,5},{2,6},{3,7},{4,0},{5,1},{6,2},{7,3},{8,12},{9,13},{10,... | collective-permute-start | bytes 491528 | tf_op jit(solution)/shard_map/ppermute | solution.py:209
  97.8 7.0 %collective-permute-done.15 = bf16[32,2560]{1,0:T(8,128)(2,1)S(1)} collective-permute-done((bf16[32,2560]{1,0:T(8,128)(2,1)S(1)}, bf16[32,2560]{1,0:T(8,128)(2,1)S(1)}, u32[]{:S(2)}, u32[]{:S(2)}) %collective-permute-start.15) | collective-permute-done | bytes 163872 | tf_op jit(solution)/shard_map/ppermute | solution.py:209
  104.9 0.9 maximum_multiply_fusion
  (29 shorter events, 0.8 us)
Async XLA Ops:
  0.6 43.2 %collective-permute-start.9 = (bf16[192,5120]{1,0:T(8,128)(2,1)}, bf16[192,5120]{1,0:T(8,128)(2,1)S(1)}, u32[]{:S(2)}, u32[]{:S(2)}) collective-permute-start(bf16[192,5120]{1,0:T(8,128)(2,1)} %tok_a.3), channel_id=1, source_target_pairs={{0,1},{1,0},{2,3},{3,2},{4,5},{5,4},{6,7},{7,6},{8,9},{9,8},{10,11... | collective-permute-start | bytes 5898248 | tf_op jit(solution)/shard_map/ppermute | solution.py:209
  2.0 1.6 %copy-start = (bf16[192,5120]{1,0:T(8,128)(2,1)S(1)}, bf16[192,5120]{1,0:T(8,128)(2,1)}, u32[]{:S(2)}) copy-start(bf16[192,5120]{1,0:T(8,128)(2,1)} %tok_a.3) | copy-start | bytes 5898244
  3.6 1.1 %copy-start.3 = (bf16[640,512]{1,0:T(8,128)(2,1)S(1)}, bf16[640,512]{1,0:T(8,128)(2,1)}, u32[]{:S(2)}) copy-start(bf16[640,512]{1,0:T(8,128)(2,1)} %code_ref.1) | copy-start | bytes 1966084
  4.7 23.2 %copy-start.2 = (bf16[192,512]{1,0:T(8,128)(2,1)S(1)}, bf16[192,512]{1,0:T(8,128)(2,1)}, u32[]{:S(2)}) copy-start(bf16[192,512]{1,0:T(8,128)(2,1)} %kg_a.7) | copy-start | bytes 589828
  6.7 19.1 %collective-permute-start.3 = (bf16[640,256]{1,0:T(8,128)(2,1)S(1)}, bf16[640,256]{1,0:T(8,128)(2,1)S(1)}, u32[]{:S(2)}, u32[]{:S(2)}) collective-permute-start(bf16[640,256]{1,0:T(8,128)(2,1)S(1)} %get-tuple-element.16.refs_0_), channel_id=1, source_target_pairs={{0,4},{1,5},{2,6},{3,7},{4,0},{5,1},{6,2},{7,3},{8,12},{9,13},{10,... | collective-permute-start | bytes 983048 | tf_op jit(solution)/shard_map/ppermute | solution.py:209
  10.4 17.1 %collective-permute-start.1 = (bf16[640,256]{1,0:T(8,128)(2,1)S(1)}, bf16[640,256]{1,0:T(8,128)(2,1)S(1)}, u32[]{:S(2)}, u32[]{:S(2)}) collective-permute-start(bf16[640,256]{1,0:T(8,128)(2,1)S(1)} %get-tuple-element.16.refs_0_), channel_id=1, source_target_pairs={{0,2},{1,3},{2,0},{3,1},{4,6},{5,7},{6,4},{7,5},{8,10},{9,11},{10,... | collective-permute-start | bytes 983048 | tf_op jit(solution)/shard_map/ppermute | solution.py:209
  25.9 10.6 %collective-permute-start.4 = (bf16[640,256]{1,0:T(8,128)(2,1)S(1)}, bf16[640,256]{1,0:T(8,128)(2,1)S(1)}, u32[]{:S(2)}, u32[]{:S(2)}) collective-permute-start(bf16[640,256]{1,0:T(8,128)(2,1)S(1)} %collective-permute-done.3.refs_4_), channel_id=1, source_target_pairs={{0,16},{16,0},{1,17},{17,1},{2,18},{18,2},{3,19},{19,3},{4,20},{20... | collective-permute-start | bytes 983048 | tf_op jit(solution)/shard_map/ppermute | solution.py:209
  27.4 14.9 %collective-permute-start.2 = (bf16[640,256]{1,0:T(8,128)(2,1)S(1)}, bf16[640,256]{1,0:T(8,128)(2,1)S(1)}, u32[]{:S(2)}, u32[]{:S(2)}) collective-permute-start(bf16[640,256]{1,0:T(8,128)(2,1)S(1)} %collective-permute-done.1.refs_2_), channel_id=1, source_target_pairs={{0,16},{16,0},{1,17},{17,1},{2,18},{18,2},{3,19},{19,3},{4,20},{20... | collective-permute-start | bytes 983048 | tf_op jit(solution)/shard_map/ppermute | solution.py:209
  27.9 1.4 %collective-permute-start = (bf16[192,512]{1,0:T(8,128)(2,1)S(1)}, bf16[192,512]{1,0:T(8,128)(2,1)S(1)}, u32[]{:S(2)}, u32[]{:S(2)}) collective-permute-start(bf16[192,512]{1,0:T(8,128)(2,1)S(1)} %copy-done.2), channel_id=1, source_target_pairs={{0,1},{1,0},{2,3},{3,2},{4,5},{5,4},{6,7},{7,6},{8,9},{9,8},{10,11... | collective-permute-start | bytes 589832 | tf_op jit(solution)/shard_map/ppermute | solution.py:209
  27.9 20.9 %collective-permute-start.6 = (bf16[640,256]{1,0:T(8,128)(2,1)S(1)}, bf16[640,256]{1,0:T(8,128)(2,1)S(1)}, u32[]{:S(2)}, u32[]{:S(2)}) collective-permute-start(bf16[640,256]{1,0:T(8,128)(2,1)S(1)} %collective-permute-done.3.refs_4_), channel_id=1, source_target_pairs={{0,2},{1,3},{2,0},{3,1},{4,6},{5,7},{6,4},{7,5},{8,10},{9,11},{10,... | collective-permute-start | bytes 983048 | tf_op jit(solution)/shard_map/ppermute | solution.py:209
  42.3 1.5 %copy-start.4 = (bf16[5120]{0:T(1024)(128)(2,1)S(1)}, bf16[5120]{0:T(1024)(128)(2,1)}, u32[]{:S(2)}) copy-start(bf16[5120]{0:T(1024)(128)(2,1)} %param.7) | copy-start | bytes 30724
  42.3 1.6 %copy-start.1 = (bf16[192,5120]{1,0:T(8,128)(2,1)S(1)}, bf16[192,5120]{1,0:T(8,128)(2,1)}, u32[]{:S(2)}) copy-start(bf16[192,5120]{1,0:T(8,128)(2,1)} %tok_a.3) | copy-start | bytes 5898244
  43.8 17.0 %collective-permute-start.5 = (bf16[192,1920]{1,0:T(8,128)(2,1)S(1)}, bf16[192,1920]{1,0:T(8,128)(2,1)S(1)}, u32[]{:S(2)}, u32[]{:S(2)}) collective-permute-start(bf16[192,1920]{1,0:T(8,128)(2,1)S(1)} %get-tuple-element.19), channel_id=1, source_target_pairs={{0,1},{1,0},{2,3},{3,2},{4,5},{5,4},{6,7},{7,6},{8,9},{9,8},{10,11... | collective-permute-start | bytes 2211848 | tf_op jit(solution)/shard_map/ppermute | solution.py:209
  47.4 19.5 %collective-permute-start.10 = (bf16[128,2560]{1,0:T(8,128)(2,1)S(1)}, bf16[128,2560]{1,0:T(8,128)(2,1)S(1)}, u32[]{:S(2)}, u32[]{:S(2)}) collective-permute-start(bf16[128,2560]{1,0:T(8,128)(2,1)S(1)} %get-tuple-element.23), channel_id=1, source_target_pairs={{0,8},{8,0},{1,9},{9,1},{2,10},{10,2},{3,11},{11,3},{4,12},{12,4},... | collective-permute-start | bytes 1966088 | tf_op jit(solution)/shard_map/ppermute | solution.py:209
  48.8 9.8 %collective-permute-start.7 = (bf16[640,256]{1,0:T(8,128)(2,1)S(1)}, bf16[640,256]{1,0:T(8,128)(2,1)S(1)}, u32[]{:S(2)}, u32[]{:S(2)}) collective-permute-start(bf16[640,256]{1,0:T(8,128)(2,1)S(1)} %collective-permute-done.6.refs_0_), channel_id=1, source_target_pairs={{0,16},{16,0},{1,17},{17,1},{2,18},{18,2},{3,19},{19,3},{4,20},{20... | collective-permute-start | bytes 983048 | tf_op jit(solution)/shard_map/ppermute | solution.py:209
  59.2 1.6 %collective-permute-start.8 = (bf16[192,640]{1,0:T(8,128)(2,1)S(1)}, bf16[192,640]{1,0:T(8,128)(2,1)S(1)}, u32[]{:S(2)}, u32[]{:S(2)}) collective-permute-start(bf16[192,640]{1,0:T(8,128)(2,1)S(1)} %get-tuple-element.21), channel_id=1, source_target_pairs={{0,1},{1,0},{2,3},{3,2},{4,5},{5,4},{6,7},{7,6},{8,9},{9,8},{10,11... | collective-permute-start | bytes 737288 | tf_op jit(solution)/shard_map/ppermute | solution.py:209
  66.2 16.9 %collective-permute-start.13 = (bf16[128,2560]{1,0:T(8,128)(2,1)S(1)}, bf16[128,2560]{1,0:T(8,128)(2,1)S(1)}, u32[]{:S(2)}, u32[]{:S(2)}) collective-permute-start(bf16[128,2560]{1,0:T(8,128)(2,1)S(1)} %get-tuple-element.27), channel_id=1, source_target_pairs={{0,8},{8,0},{1,9},{9,1},{2,10},{10,2},{3,11},{11,3},{4,12},{12,4},... | collective-permute-start | bytes 1966088 | tf_op jit(solution)/shard_map/ppermute | solution.py:209
  67.1 17.2 %collective-permute-start.11 = (bf16[64,2560]{1,0:T(8,128)(2,1)S(1)}, bf16[64,2560]{1,0:T(8,128)(2,1)S(1)}, u32[]{:S(2)}, u32[]{:S(2)}) collective-permute-start(bf16[64,2560]{1,0:T(8,128)(2,1)S(1)} %slice.53), channel_id=1, source_target_pairs={{0,2},{1,3},{2,0},{3,1},{4,6},{5,7},{6,4},{7,5},{8,10},{9,11},{10,... | collective-permute-start | bytes 983048 | tf_op jit(solution)/shard_map/ppermute | solution.py:209
  83.2 12.5 %collective-permute-start.14 = (bf16[64,2560]{1,0:T(8,128)(2,1)S(1)}, bf16[64,2560]{1,0:T(8,128)(2,1)S(1)}, u32[]{:S(2)}, u32[]{:S(2)}) collective-permute-start(bf16[64,2560]{1,0:T(8,128)(2,1)S(1)} %slice.52), channel_id=1, source_target_pairs={{0,2},{1,3},{2,0},{3,1},{4,6},{5,7},{6,4},{7,5},{8,10},{9,11},{10,... | collective-permute-start | bytes 983048 | tf_op jit(solution)/shard_map/ppermute | solution.py:209
  84.4 13.4 %collective-permute-start.12 = (bf16[32,2560]{1,0:T(8,128)(2,1)S(1)}, bf16[32,2560]{1,0:T(8,128)(2,1)S(1)}, u32[]{:S(2)}, u32[]{:S(2)}) collective-permute-start(bf16[32,2560]{1,0:T(8,128)(2,1)S(1)} %slice.55), channel_id=1, source_target_pairs={{0,4},{1,5},{2,6},{3,7},{4,0},{5,1},{6,2},{7,3},{8,12},{9,13},{10,... | collective-permute-start | bytes 491528 | tf_op jit(solution)/shard_map/ppermute | solution.py:209
  95.8 9.0 %collective-permute-start.15 = (bf16[32,2560]{1,0:T(8,128)(2,1)S(1)}, bf16[32,2560]{1,0:T(8,128)(2,1)S(1)}, u32[]{:S(2)}, u32[]{:S(2)}) collective-permute-start(bf16[32,2560]{1,0:T(8,128)(2,1)S(1)} %slice.54), channel_id=1, source_target_pairs={{0,4},{1,5},{2,6},{3,7},{4,0},{5,1},{6,2},{7,3},{8,12},{9,13},{10,... | collective-permute-start | bytes 491528 | tf_op jit(solution)/shard_map/ppermute | solution.py:209

commit v2 on v1

v2 whole, which is shorter than its diff:
```python
import functools
import math

import jax
import jax.numpy as jnp
from jax import lax
from jax.experimental import pallas as pl
from jax.experimental.pallas import tpu as pltpu
from jax.sharding import PartitionSpec as P

F32, BF16 = jnp.float32, jnp.bfloat16
EPS = 1e-06
ROWS = 16
STAGES = 4
COST_D = 20000000000.0
COST_P = 0
COST_Q = 0
COST_T = 0
DIRECT = False
CUTS = (768, 2304, 2048)
GROUPS = ((2304,), (2048,))
EVENTS = ('u1', 'u2', 'd0', 'u3', 'f1', 'g1', 'F0', 'd2', 'p', 'F1', 'q', 'F2', 't')
NT = (((1,), (1,)), ((), ()))


def general(tokens, key_grad, gain, key_codes, code_scales):
    row_count = tokens.shape[0]
    feature_count = tokens.shape[1]
    key_width = key_codes.shape[1]
    group_cols = key_width // code_scales.shape[1]
    values = tokens.astype(F32)
    inverse_rms = lax.rsqrt(jnp.mean(values * values, axis=1, keepdims=True) + EPS)
    unit_rows = values * inverse_rms
    gain_wide = gain.astype(F32)
    normed = (unit_rows * gain_wide).astype(BF16)
    weight_shard = (
        key_codes.astype(F32) * jnp.repeat(code_scales.astype(F32), group_cols, axis=1)
    ).astype(BF16)
    product = lax.dot_general(
        key_grad,
        lax.all_gather(weight_shard, "narrow", axis=0, tiled=True),
        NT,
        preferred_element_type=F32,
    )
    scaled = product * gain_wide
    inner_mean = jnp.mean(scaled * unit_rows, axis=1, keepdims=True)
    token_grad = (inverse_rms * (scaled - unit_rows * inner_mean)).astype(BF16)
    term = lax.dot_general(
        key_grad, normed, (((0,), (0,)), ((), ())), preferred_element_type=F32
    ).astype(BF16)
    wide_count = lax.axis_size("wide")
    narrow_count = lax.axis_size("narrow")
    column_block = key_width // (wide_count * narrow_count)
    blocks = term.reshape(wide_count, narrow_count, column_block, feature_count)
    received = lax.all_to_all(blocks, "narrow", split_axis=1, concat_axis=1, tiled=True)
    partial_value = jnp.sum(received.astype(F32), axis=1)
    owned = lax.all_to_all(partial_value, "wide", split_axis=0, concat_axis=0, tiled=True)
    summed = jnp.sum(owned, axis=0)
    token_total = row_count * wide_count * narrow_count
    weight_grad = summed / math.sqrt(token_total)
    return (token_grad, weight_grad)


def call(kernel, out_shape, scratch=(), n_in=1, far_in=(), far_out=False, limit=16, flops=0, name=None):
    vmem = pl.BlockSpec(memory_space=pltpu.VMEM)
    anywhere = pl.BlockSpec(memory_space=pltpu.HBM)
    return pl.pallas_call(
        kernel,
        out_shape=out_shape,
        in_specs=[anywhere if i in far_in else vmem for i in range(n_in)],
        out_specs=jax.tree.map(lambda _: anywhere if far_out else vmem, out_shape),
        scratch_shapes=list(scratch),
        compiler_params=pltpu.CompilerParams(vmem_limit_bytes=limit * 2**20),
        cost_estimate=pl.CostEstimate(flops=int(flops), bytes_accessed=0, transcendentals=0),
        name=name,
    )


def fetch(sources, targets, sems):
    copies = [pltpu.make_async_copy(a, b, sems.at[n]) for n, (a, b) in enumerate(zip(sources, targets))]
    for copy in copies:
        copy.start()
    return copies


def arrived(copies):
    for copy in copies:
        copy.wait()


def inverse_rms_into(tok_ref, inv_ref):
    rows, width = tok_ref.shape

    def step(i, carry):
        r = pl.ds(pl.multiple_of(i * ROWS, ROWS), ROWS)
        totals = [jnp.zeros((ROWS, 128), F32)] * 4
        for j in range(width // 128):
            v = tok_ref[r, j * 128 : (j + 1) * 128].astype(F32)
            totals[j % 4] = totals[j % 4] + v * v
        inv_ref[r, :] = (totals[0] + totals[1]) + (totals[2] + totals[3])
        return carry

    lax.fori_loop(0, rows // ROWS, step, 0)
    mean = jnp.sum(inv_ref[...], axis=1, keepdims=True) * (1.0 / width)
    inv_ref[...] = jnp.broadcast_to(lax.rsqrt(mean + EPS), inv_ref.shape)


def decode_kernel(code_hbm, scale_hbm, sent_ref, kept_ref, code_ref, scale_ref, sems):
    arrived(fetch((code_hbm, scale_hbm), (code_ref, scale_ref), sems))
    groups = scale_ref.shape[0]
    cols = code_ref.shape[1] // groups
    side = lax.axis_index("parts")
    half = groups // 2
    scales = scale_ref[...].astype(F32).T
    for g in range(groups):
        block = (code_ref[:, g * cols : (g + 1) * cols].astype(F32) * scales[:, g : g + 1]).astype(BF16)
        at = (g % half) * cols

        @pl.when(side == g // half)
        def _():
            sent_ref[:, at : at + cols] = block

        @pl.when(side != g // half)
        def _():
            kept_ref[:, at : at + cols] = block


def pick_rows(kg_a, kg_b, picked):
    rows, keys = kg_a.shape
    wide, spot = lax.axis_index("wide"), lax.axis_index("narrow")
    z, core = spot // 2, spot % 2
    row = lax.broadcasted_iota(jnp.int32, (256, 1), 0)
    col = lax.broadcasted_iota(jnp.int32, (256, keys), 1)
    group = row // 32
    order = group % 4
    apart = (order % 2) * 2 + order // 2
    target = 256 * jnp.where(group < 4, 1 - wide, wide) + 64 * (apart ^ z) + 32 * core + row % 32
    pick = jnp.where(col == target, 1.0, 0.0).astype(BF16)
    for n, kg in enumerate((kg_a, kg_b)):
        picked[:, n * rows : (n + 1) * rows] = lax.dot_general(pick, kg[...], NT, preferred_element_type=F32).astype(BF16)


def normed_into(tok, inv, gain, first, count, normed, base):
    def step(i, carry):
        at = pl.multiple_of(i * ROWS, ROWS)
        scale = inv[pl.ds(at, ROWS), :]
        for j in range(0, count, 128):
            v = tok[pl.ds(at, ROWS), first + j : first + j + 128].astype(F32)
            g = gain[(first + j) // 128 : (first + j) // 128 + 1, :]
            normed[pl.ds(base + at, ROWS), j : j + 128] = (v * scale * g).astype(BF16)
        return carry

    lax.fori_loop(0, tok.shape[0] // ROWS, step, 0)


def term_into(picked, normed, sent_ref, kept_ref, first):
    count = sent_ref.shape[1]
    tile = 512 if count % 512 == 0 else 256
    for j in range(0, count, tile):
        term = jnp.dot(picked[...], normed[:, first + j : first + j + tile], preferred_element_type=F32).astype(BF16)
        sent_ref[:, j : j + tile] = term[:128]
        kept_ref[:, j : j + tile] = term[128:]


def first_term_kernel(
    tok_hbm, kg_hbm, gain_hbm, tok_b, kg_b, sent_ref, kept_ref, inv_a, inv_b, picked, tok_a, kg_a, normed, gain_ref, gain, sems
):
    rows = tok_b.shape[0]
    small = fetch((kg_hbm, gain_hbm), (kg_a, gain_ref), sems)
    large = fetch((tok_hbm,), (tok_a,), sems.at[2:])
    inverse_rms_into(tok_b, inv_b)
    arrived(small)
    gain[...] = gain_ref[...].astype(F32)
    pick_rows(kg_a, kg_b, picked)
    arrived(large)
    inverse_rms_into(tok_a, inv_a)
    count = sent_ref.shape[1]
    normed_into(tok_a, inv_a, gain, 0, count, normed, 0)
    normed_into(tok_b, inv_b, gain, 0, count, normed, rows)
    term_into(picked, normed, sent_ref, kept_ref, 0)


def more_terms_kernel(first, tok_hbm, gain_hbm, tok_b, inv_a, inv_b, picked, *refs):
    outs, (tok_a, normed, gain_ref, gain, sems) = refs[:-5], refs[-5:]
    rows = tok_b.shape[0]
    small = fetch((gain_hbm,), (gain_ref,), sems)
    large = fetch((tok_hbm,), (tok_a,), sems.at[1:])
    arrived(small)
    gain[...] = gain_ref[...].astype(F32)
    count = normed.shape[1]
    normed_into(tok_b, inv_b, gain, first, count, normed, rows)
    arrived(large)
    normed_into(tok_a, inv_a, gain, first, count, normed, 0)
    at = 0
    for sent_ref, kept_ref in zip(outs[::2], outs[1::2]):
        term_into(picked, normed, sent_ref, kept_ref, at)
        at += sent_ref.shape[1]


def product_kernel(blocks, kg_a, kg_b, *refs):
    parts, (own_ref, sent_ref) = refs[: 2 * blocks], refs[2 * blocks :]
    side = lax.axis_index("parts")
    half = kg_a.shape[1] // 2
    near = pl.ds(pl.multiple_of(side * half, half), half)
    far = pl.ds(pl.multiple_of((1 - side) * half, half), half)
    width = parts[0].shape[0]
    for kg, out in ((kg_b, sent_ref), (kg_a, own_ref)):
        a, b = kg[:, near], kg[:, far]
        for n in range(blocks):
            value = lax.dot_general(a, parts[2 * n][...], NT, preferred_element_type=F32)
            value = value + lax.dot_general(b, parts[2 * n + 1][...], NT, preferred_element_type=F32)
            out[:, n * width : (n + 1) * width] = value.astype(out.dtype)


def token_kernel(counts, tok_hbm, gain_hbm, inv_ref, *refs):
    pieces, (out_hbm, out_ref, scaled_ref, tok_ref, total_ref, gain_ref, gain, sems) = refs[:-8], refs[-8:]
    arrived(fetch((gain_hbm, tok_hbm), (gain_ref, tok_ref), sems))
    rows, width = tok_ref.shape
    gain[...] = gain_ref[...].astype(F32)
    spot = lax.axis_index("narrow")
    z, core = spot // 2, spot % 2
    block = width // 8
    table = []
    k = 0
    for p, count in enumerate(counts):
        for n in range(count):
            for m in range(2):
                who = core if m == 0 else 1 - core
                table.append((pieces[2 * p + m], n * block, 2 * (z ^ k) + who, (2 * k + m) * block))
            k += 1

    def weigh(i, carry):
        r = pl.ds(pl.multiple_of(i * ROWS, ROWS), ROWS)
        totals = [jnp.zeros((ROWS, 128), F32)] * 4
        for ref, start, where, keep in table:
            for j in range(block // 128):
                spot = where * (block // 128) + j
                scaled = ref[r, start + j * 128 : start + j * 128 + 128].astype(F32) * gain[pl.ds(spot, 1), :]
                scaled_ref[r, keep + j * 128 : keep + j * 128 + 128] = scaled
                unit = tok_ref[r, pl.ds(pl.multiple_of(spot * 128, 128), 128)].astype(F32)
                totals[j % 4] = totals[j % 4] + scaled * unit
        total_ref[r, :] = ((totals[0] + totals[1]) + (totals[2] + totals[3])) * inv_ref[r, :]
        return carry

    lax.fori_loop(0, rows // ROWS, weigh, 0)
    mean = jnp.sum(total_ref[...], axis=1, keepdims=True) * (1.0 / width)
    total_ref[...] = jnp.broadcast_to(mean, total_ref.shape)

    def write(i, carry):
        r = pl.ds(pl.multiple_of(i * ROWS, ROWS), ROWS)
        inv = inv_ref[r, :]
        mean = total_ref[r, :]
        for ref, start, where, keep in table:
            for j in range(block // 128):
                lanes = pl.ds(pl.multiple_of((where * (block // 128) + j) * 128, 128), 128)
                unit = tok_ref[r, lanes].astype(F32) * inv
                scaled = scaled_ref[r, keep + j * 128 : keep + j * 128 + 128]
                out_ref[r, lanes] = (inv * (scaled - unit * mean)).astype(BF16)
        return carry

    stage = rows // STAGES
    copies = []
    for n in range(STAGES):
        lax.fori_loop(n * stage // ROWS, (n + 1) * stage // ROWS, write, 0)
        r = pl.ds(n * stage, stage)
        copies.append(pltpu.make_async_copy(out_ref.at[r], out_hbm.at[r], sems.at[2 + n]))
        copies[-1].start()
    arrived(copies)


def swap_pairs(count, bit):
    return [(i, i ^ bit) for i in range(count)]


def after(value, earlier):
    return lax.optimization_barrier((value, earlier))[0]


def tuned(tokens, key_grad, gain, key_codes, code_scales):
    rows, width = tokens.shape
    keys = key_grad.shape[1]
    S = jax.ShapeDtypeStruct
    swap = lambda a, axis, bit: lax.ppermute(a, axis, swap_pairs(lax.axis_size(axis), bit))
    core = lambda a: swap(a, "narrow", 1)
    near = lambda a: swap(a, "narrow", 2)
    far = lambda a: swap(a, "narrow", 4)
    across = lambda a: swap(a, "wide", 1)
    opposite = lambda a: swap(a, "narrow", 6)
    beside = lambda a: swap(a, "parts", 1)
    shard = key_codes.shape[0]

    tok_b, kg_b = core(tokens), core(key_grad)
    unit, rest = call(
        decode_kernel,
        (S((shard, keys // 2), BF16),) * 2,
        scratch=(
            pltpu.VMEM(key_codes.shape, BF16),
            pltpu.VMEM(code_scales.shape[::-1], BF16),
            pltpu.SemaphoreType.DMA((2,)),
        ),
        n_in=2, far_in=(0, 1), flops=COST_D, name="decode",
    )(key_codes, code_scales.T)
    units = {1: near(unit), 2: far(unit)}
    if DIRECT:
        units[3] = opposite(unit)

    gain_row = gain.reshape(width // 128, 128)
    cuts = CUTS
    inv = S((rows, 128), F32)
    gains = pltpu.VMEM((width // 128, 128), BF16), pltpu.VMEM((width // 128, 128), F32)
    whole = pltpu.VMEM((rows, width), BF16)
    *pair, inv_a, inv_b, picked = call(
        first_term_kernel,
        (S((128, cuts[0]), BF16),) * 2 + (inv, inv, S((256, 2 * rows), BF16)),
        scratch=(
            whole,
            pltpu.VMEM((rows, keys), BF16),
            pltpu.VMEM((2 * rows, cuts[0]), BF16),
            *gains,
            pltpu.SemaphoreType.DMA((3,)),
        ),
        n_in=5, far_in=(0, 1, 2), name="first_term",
    )(tokens, key_grad, gain_row, tok_b, after(kg_b, unit))
    pairs, first = pair, cuts[0]
    for group in GROUPS:
        total = sum(group)
        pairs = pairs + list(
            call(
                functools.partial(more_terms_kernel, first),
                tuple(S((128, cut), BF16) for cut in group for _ in range(2)),
                scratch=(whole, pltpu.VMEM((2 * rows, total), BF16), *gains, pltpu.SemaphoreType.DMA((2,))),
                n_in=6, far_in=(0, 1), name="more_terms",
            )(tokens, gain_row, tok_b, inv_a, inv_b, after(picked, pairs[-1]))
        )
        first += total
    sent, kept = pairs[::2], pairs[1::2]

    got = [across(a) for a in sent]
    scale = 1 / math.sqrt(rows * lax.axis_size("wide") * lax.axis_size("narrow"))
    marker = [sent[-1]]

    def then(value):
        return after(value, marker[0])

    def mark(value):
        marker[0] = value
        return value

    def product(cost, *parts):
        n = len(parts) // 2
        own, sent = call(
            functools.partial(product_kernel, n),
            (S((rows, n * shard), F32), S((rows, n * shard), BF16)),
            n_in=2 + 2 * n, flops=cost, name="product",
        )(key_grad, kg_b, *parts)
        return own, mark(sent)

    totals, received, owned = {}, {}, {}

    def fold(n):
        a, b = then((kept[n], got[n]))
        total = a.astype(F32) + b.astype(F32)
        totals[n] = total[:64]
        received[n] = near(mark(total[64:].astype(BF16)))

    def fold_again(n):
        total = totals[n] + then(received[n]).astype(F32)
        totals[n] = total[:32]
        received[n] = far(mark(total[32:].astype(BF16)))

    def spread(n):
        a, b = then((kept[n], got[n]))
        total = a.astype(F32) + b.astype(F32)
        totals[n] = total[:32]
        pieces = mark([total[32 * i : 32 * i + 32].astype(BF16) for i in range(1, 4)])
        received[n] = far(pieces[0]), near(pieces[1]), opposite(pieces[2])

    def finish(n):
        arrived = received[n] if isinstance(received[n], tuple) else (received[n],)
        total = totals[n]
        for a in then(arrived):
            total = total + a.astype(F32)
        owned[n] = mark(total * scale)

    others = {}

    def arrive(k):
        units[k] = mark(then(units[k]))
        others[k] = beside(units[k])
        if k == 2 and not DIRECT:
            units[3] = near(units[k])

    most = last = None
    for event in EVENTS:
        kind, n = event[0], int(event[1:] or 0)
        if kind == "u":
            arrive(n)
        elif kind == "f":
            fold(n)
        elif kind == "g":
            fold_again(n)
        elif kind == "d":
            spread(n)
        elif kind == "p":
            own, other = product(COST_P, *then((unit, rest, units[1], others[1], units[2], others[2])))
            most = own, core(other)
        elif kind == "q":
            own, other = product(COST_Q, *then((units[3], others[3])))
            last = own, core(other)
        elif kind == "F":
            finish(n)
        elif kind == "t":
            token_grad = call(
                functools.partial(token_kernel, (3, 1)),
                S((rows, width), BF16),
                scratch=(
                    whole,
                    pltpu.VMEM((rows, width), F32),
                    whole,
                    pltpu.VMEM((rows, 128), F32),
                    *gains,
                    pltpu.SemaphoreType.DMA((2 + STAGES,)),
                ),
                n_in=7, far_in=(0, 1), far_out=True, flops=COST_T, name="token_grad",
            )(tokens, gain_row, inv_a, *then((most, last))[0], *last)
            mark(token_grad)
    weight_grad = jnp.concatenate([owned[n] for n in range(len(cuts))], axis=1)
    return (token_grad, weight_grad)


def solution(mesh):
    sizes = dict(mesh.shape)
    fits = sizes["parts"] == 2 and sizes["wide"] == 2 and sizes["narrow"] == 8
    return jax.shard_map(
        tuned if fits else general,
        mesh=mesh,
        in_specs=(
            P(("parts", "wide", "narrow"), None),
            P(("parts", "wide", "narrow"), None),
            P(),
            P("narrow", None),
            P("narrow", None),
        ),
        out_specs=(P(("parts", "wide", "narrow"), None), P(("parts", "wide", "narrow"), None)),
        check_vma=False,
    )
```

time: 106 us -> 65.5 us (0.62)
  waiting for transfers between devices: 66.9 us -> 21.8 us
  starting transfers between devices: 20.1 us -> 27.1 us
  local copies, waits for them, and re-layouts: 3.66 us -> 1.88 us
    ppermute x16 -> x21, waiting for transfers between devices: 66.9 us -> 21.8 us  [tuned(): lax.ppermute(a, axis, swap_pairs(lax.axis_size(axis), bit))]
    ppermute x16 -> x21, starting transfers between devices: 20.1 us -> 27.1 us  [tuned(): lax.ppermute(a, axis, swap_pairs(lax.axis_size(axis), bit))]
    unnamed x11 -> x10, local copies, waits for them, and re-layouts: 3.54 us -> 1.79 us
    pallas_call x3 -> x4, Pallas kernels: 7.09 us -> 7.21 us  [the longest x2 3.24 us: tuned(): call(functools.partial(more_terms_kernel, first), tuple((S((128, cut), BF...]
  transfers between devices with their start and end apart: 16 -> 21, of which waited for: 9 -> 9; matrix products, arithmetic and copies ran while one was open for 1% -> 2% of each run, Pallas kernels for 12% -> 14%
where the time goes in v2:
time: 65.5 us; the launch traced here: 65.3 us
  starting transfers between devices  27.1 us (41%)
  waiting for transfers between devices  21.8 us (33%)
  Pallas kernels  12.4 us (19%)
  local copies, waits for them, and re-layouts  1.88 us (3%)
  other arithmetic  1.39 us (2%)
  between operations  0.79 us (1%)
    ppermute x21, starting transfers between devices, tuned(): lax.ppermute(a, axis, swap_pairs(lax.axis_size(axis), bit))  27.1 us
    ppermute x21, waiting for transfers between devices, tuned(): lax.ppermute(a, axis, swap_pairs(lax.axis_size(axis), bit))  21.8 us
    pallas_call x2, Pallas kernels, tuned(): call(functools.partial(more_terms_kernel, first), tuple((S((128, cut), BF...  3.24 us
    pallas_call x1, Pallas kernels, tuned(): call(functools.partial(token_kernel, (3, 1)), S((rows, width), BF16), scr...  3.19 us
    pallas_call x1, Pallas kernels, tuned(): call(first_term_kernel, (S((128, cuts[0]), BF16),) * 2 + (inv, inv, S((25...  2.95 us
    pallas_call x2, Pallas kernels, product(): call(functools.partial(product_kernel, n), (S((rows, n * shard), F32), S(...  1.97 us
    unnamed x10, local copies, waits for them, and re-layouts  1.79 us
  transfers between devices with their start and end apart: 21, of which 9 were waited for; matrix products, arithmetic and copies ran while one was open for 2% of the time, Pallas kernels for 14%

profile of v2, /device:TPU:0, one launch (start us, length us, event | category | flops | bytes accessed | tf_op | source)
XLA Modules:
  0.0 65.3 jit_solution(5415934597596214051)
XLA Ops:
  1.2 1.1 %copy-done.3 = bf16[640,512]{1,0:T(8,128)(2,1)S(1)} copy-done((bf16[640,512]{1,0:T(8,128)(2,1)S(1)}, bf16[640,512]{1,0:T(8,128)(2,1)}, u32[]{:S(2)}) %copy-start.3) | copy-done | bytes 655384
  2.3 0.7 %copy-done.4 = bf16[640,4]{0,1:T(4,128)(2,1)S(1)} copy-done((bf16[640,4]{0,1:T(4,128)(2,1)S(1)}, bf16[640,4]{0,1:T(4,128)(2,1)}, u32[]{:S(2)}) %copy-start.4) | copy-done | bytes 5144
  3.0 1.0 %decode.1 = (bf16[640,256]{1,0:T(8,128)(2,1)S(1)}, bf16[640,256]{1,0:T(8,128)(2,1)S(1)}) custom-call(bf16[640,512]{1,0:T(8,128)(2,1)S(1)} %copy-done.3, bf16[4,640]{1,0:T(4,128)(2,1)S(1)} %bitcast.6), custom_call_target="tpu_custom_call" | custom-call | flops 20000000000 | tf_op jit(solution)/shard_map/decode/pallas_call | solution.py:293
  4.0 3.1 %collective-permute-start.2 = (bf16[640,256]{1,0:T(8,128)(2,1)S(1)}, bf16[640,256]{1,0:T(8,128)(2,1)S(1)}, u32[]{:S(2)}, u32[]{:S(2)}) collective-permute-start(bf16[640,256]{1,0:T(8,128)(2,1)S(1)} %get-tuple-element.74.refs_0_), channel_id=1, source_target_pairs={{0,2},{1,3},{2,0},{3,1},{4,6},{5,7},{6,4},{7,5},{8,10},{9,11},{10,... | collective-permute-start | bytes 983048 | tf_op jit(solution)/shard_map/ppermute | solution.py:283
  7.1 2.6 %collective-permute-start.4 = (bf16[640,256]{1,0:T(8,128)(2,1)S(1)}, bf16[640,256]{1,0:T(8,128)(2,1)S(1)}, u32[]{:S(2)}, u32[]{:S(2)}) collective-permute-start(bf16[640,256]{1,0:T(8,128)(2,1)S(1)} %get-tuple-element.74.refs_0_), channel_id=1, source_target_pairs={{0,4},{1,5},{2,6},{3,7},{4,0},{5,1},{6,2},{7,3},{8,12},{9,13},{10,... | collective-permute-start | bytes 983048 | tf_op jit(solution)/shard_map/ppermute | solution.py:283
  9.7 3.0 %first_term.1 = (bf16[128,768]{1,0:T(8,128)(2,1)S(1)}, bf16[128,768]{1,0:T(8,128)(2,1)S(1)}, f32[192,128]{1,0:T(8,128)S(1)}, f32[192,128]{1,0:T(8,128)S(1)}, bf16[256,384]{1,0:T(8,128)(2,1)S(1)}) custom-call(bf16[192,5120]{1,0:T(8,128)(2,1)S(1)} %copy-done, bf16[192,512]{1,0:T(8,128)(2,1)S(1)} %copy-done.1, bf16[40,128]{1,0:T(8,128)(2,1)S(1)} %bitcast.2, ...), custom_call_target="tpu_custom_call" | custom-call | tf_op jit(solution)/shard_map/first_term/pallas_call | solution.py:312
  12.7 1.6 %collective-permute-start.7 = (bf16[128,768]{1,0:T(8,128)(2,1)S(1)}, bf16[128,768]{1,0:T(8,128)(2,1)S(1)}, u32[]{:S(2)}, u32[]{:S(2)}) collective-permute-start(bf16[128,768]{1,0:T(8,128)(2,1)S(1)} %get-tuple-element.61), channel_id=1, source_target_pairs={{0,8},{8,0},{1,9},{9,1},{2,10},{10,2},{3,11},{11,3},{4,12},{12,4},... | collective-permute-start | bytes 589832 | tf_op jit(solution)/shard_map/ppermute | solution.py:283
  14.2 1.7 %more_terms.2 = (bf16[128,2304]{1,0:T(8,128)(2,1)S(1)}, bf16[128,2304]{1,0:T(8,128)(2,1)S(1)}) custom-call(bf16[192,5120]{1,0:T(8,128)(2,1)S(1)} %copy-done, bf16[40,128]{1,0:T(8,128)(2,1)S(1)} %bitcast.3, bf16[192,5120]{1,0:T(8,128)(2,1)S(1)} %collective-permute-done.tok_b, f32[192,128]{1,0:T(8,128)S(1)} %get-tuple-element.49.inv_a.inv_ref, ...), custom_call_target="tpu_custom_call" | custom-call | tf_op jit(solution)/shard_map/more_terms/pallas_call | solution.py:328
  15.9 0.6 collective-permute-start.11
  16.5 1.6 %more_terms.3 = (bf16[128,2048]{1,0:T(8,128)(2,1)S(1)}, bf16[128,2048]{1,0:T(8,128)(2,1)S(1)}) custom-call(bf16[192,5120]{1,0:T(8,128)(2,1)S(1)} %copy-done, bf16[40,128]{1,0:T(8,128)(2,1)S(1)} %bitcast.4, bf16[192,5120]{1,0:T(8,128)(2,1)S(1)} %collective-permute-done.tok_b, f32[192,128]{1,0:T(8,128)S(1)} %get-tuple-element.49.inv_a.inv_ref, ...), custom_call_target="tpu_custom_call" | custom-call | tf_op jit(solution)/shard_map/more_terms/pallas_call | solution.py:328
  18.1 3.9 %collective-permute-done.2.refs_2_ = bf16[640,256]{1,0:T(8,128)(2,1)S(1)} collective-permute-done((bf16[640,256]{1,0:T(8,128)(2,1)S(1)}, bf16[640,256]{1,0:T(8,128)(2,1)S(1)}, u32[]{:S(2)}, u32[]{:S(2)}) %collective-permute-start.2) | collective-permute-done | bytes 327712 | tf_op jit(solution)/shard_map/ppermute | solution.py:283
  22.0 2.5 %collective-permute-done.4.refs_4_ = bf16[640,256]{1,0:T(8,128)(2,1)S(1)} collective-permute-done((bf16[640,256]{1,0:T(8,128)(2,1)S(1)}, bf16[640,256]{1,0:T(8,128)(2,1)S(1)}, u32[]{:S(2)}, u32[]{:S(2)}) %collective-permute-start.4) | collective-permute-done | bytes 327712 | tf_op jit(solution)/shard_map/ppermute | solution.py:283
  25.0 7.0 %collective-permute-done.12.refs_0_ = bf16[640,256]{1,0:T(8,128)(2,1)S(1)} collective-permute-done((bf16[640,256]{1,0:T(8,128)(2,1)S(1)}, bf16[640,256]{1,0:T(8,128)(2,1)S(1)}, u32[]{:S(2)}, u32[]{:S(2)}) %collective-permute-start.12) | collective-permute-done | bytes 327712 | tf_op jit(solution)/shard_map/ppermute | solution.py:283
  32.2 1.8 %collective-permute-start.13 = (bf16[64,2304]{1,0:T(8,128)(2,1)S(1)}, bf16[64,2304]{1,0:T(8,128)(2,1)S(1)}, u32[]{:S(2)}, u32[]{:S(2)}) collective-permute-start(bf16[64,2304]{1,0:T(8,128)(2,1)S(1)} %slice.88), channel_id=1, source_target_pairs={{0,2},{1,3},{2,0},{3,1},{4,6},{5,7},{6,4},{7,5},{8,10},{9,11},{10,... | collective-permute-start | bytes 884744 | tf_op jit(solution)/shard_map/ppermute | solution.py:283
  34.0 1.5 %collective-permute-start.6 = (bf16[128,2048]{1,0:T(8,128)(2,1)S(1)}, bf16[128,2048]{1,0:T(8,128)(2,1)S(1)}, u32[]{:S(2)}, u32[]{:S(2)}) collective-permute-start(bf16[128,2048]{1,0:T(8,128)(2,1)S(1)} %get-tuple-element.57), channel_id=1, source_target_pairs={{0,8},{8,0},{1,9},{9,1},{2,10},{10,2},{3,11},{11,3},{4,12},{12,4},... | collective-permute-start | bytes 1572872 | tf_op jit(solution)/shard_map/ppermute | solution.py:283
  35.5 1.5 %collective-permute-start.5 = (bf16[640,256]{1,0:T(8,128)(2,1)S(1)}, bf16[640,256]{1,0:T(8,128)(2,1)S(1)}, u32[]{:S(2)}, u32[]{:S(2)}) collective-permute-start(bf16[640,256]{1,0:T(8,128)(2,1)S(1)} %collective-permute-done.4.refs_4_), channel_id=1, source_target_pairs={{0,16},{16,0},{1,17},{17,1},{2,18},{18,2},{3,19},{19,3},{4,20},{20... | collective-permute-start | bytes 983048 | tf_op jit(solution)/shard_map/ppermute | solution.py:283
  37.0 2.1 %collective-permute-start.10 = (bf16[32,768]{1,0:T(8,128)(2,1)S(1)}, bf16[32,768]{1,0:T(8,128)(2,1)S(1)}, u32[]{:S(2)}, u32[]{:S(2)}) collective-permute-start(bf16[32,768]{1,0:T(8,128)(2,1)S(1)} %get-tuple-element.99), channel_id=1, source_target_pairs={{0,6},{1,7},{2,4},{3,5},{4,2},{5,3},{6,0},{7,1},{8,14},{9,15},{10,... | collective-permute-start | bytes 147464 | tf_op jit(solution)/shard_map/ppermute | solution.py:283
  39.3 1.8 %collective-permute-done.13 = bf16[64,2304]{1,0:T(8,128)(2,1)S(1)} collective-permute-done((bf16[64,2304]{1,0:T(8,128)(2,1)S(1)}, bf16[64,2304]{1,0:T(8,128)(2,1)S(1)}, u32[]{:S(2)}, u32[]{:S(2)}) %collective-permute-start.13) | collective-permute-done | bytes 294944 | tf_op jit(solution)/shard_map/ppermute | solution.py:283
  41.2 1.6 %collective-permute-start.9 = (bf16[32,768]{1,0:T(8,128)(2,1)S(1)}, bf16[32,768]{1,0:T(8,128)(2,1)S(1)}, u32[]{:S(2)}, u32[]{:S(2)}) collective-permute-start(bf16[32,768]{1,0:T(8,128)(2,1)S(1)} %get-tuple-element.100), channel_id=1, source_target_pairs={{0,2},{1,3},{2,0},{3,1},{4,6},{5,7},{6,4},{7,5},{8,10},{9,11},{10,... | collective-permute-start | bytes 147464 | tf_op jit(solution)/shard_map/ppermute | solution.py:283
  43.4 1.6 %collective-permute-start.3 = (bf16[640,256]{1,0:T(8,128)(2,1)S(1)}, bf16[640,256]{1,0:T(8,128)(2,1)S(1)}, u32[]{:S(2)}, u32[]{:S(2)}) collective-permute-start(bf16[640,256]{1,0:T(8,128)(2,1)S(1)} %collective-permute-done.2.refs_2_), channel_id=1, source_target_pairs={{0,16},{16,0},{1,17},{17,1},{2,18},{18,2},{3,19},{19,3},{4,20},{20... | collective-permute-start | bytes 983048 | tf_op jit(solution)/shard_map/ppermute | solution.py:283
  45.0 0.6 collective-permute-start.15
  45.8 2.2 %collective-permute-start.16 = (bf16[32,2304]{1,0:T(8,128)(2,1)S(1)}, bf16[32,2304]{1,0:T(8,128)(2,1)S(1)}, u32[]{:S(2)}, u32[]{:S(2)}) collective-permute-start(bf16[32,2304]{1,0:T(8,128)(2,1)S(1)} %slice.89), channel_id=1, source_target_pairs={{0,4},{1,5},{2,6},{3,7},{4,0},{5,1},{6,2},{7,3},{8,12},{9,13},{10,... | collective-permute-start | bytes 442376 | tf_op jit(solution)/shard_map/ppermute | solution.py:283
  48.3 0.7 %collective-permute-start.18 = (bf16[32,2048]{1,0:T(8,128)(2,1)S(1)}, bf16[32,2048]{1,0:T(8,128)(2,1)S(1)}, u32[]{:S(2)}, u32[]{:S(2)}) collective-permute-start(bf16[32,2048]{1,0:T(8,128)(2,1)S(1)} %get-tuple-element.96), channel_id=1, source_target_pairs={{0,4},{1,5},{2,6},{3,7},{4,0},{5,1},{6,2},{7,3},{8,12},{9,13},{10,... | collective-permute-start | bytes 393224 | tf_op jit(solution)/shard_map/ppermute | solution.py:283
  49.0 1.5 %collective-permute-start.19 = (bf16[32,2048]{1,0:T(8,128)(2,1)S(1)}, bf16[32,2048]{1,0:T(8,128)(2,1)S(1)}, u32[]{:S(2)}, u32[]{:S(2)}) collective-permute-start(bf16[32,2048]{1,0:T(8,128)(2,1)S(1)} %get-tuple-element.95), channel_id=1, source_target_pairs={{0,2},{1,3},{2,0},{3,1},{4,6},{5,7},{6,4},{7,5},{8,10},{9,11},{10,... | collective-permute-start | bytes 393224 | tf_op jit(solution)/shard_map/ppermute | solution.py:283
  50.5 2.8 %collective-permute-done.3.refs_3_ = bf16[640,256]{1,0:T(8,128)(2,1)S(1)} collective-permute-done((bf16[640,256]{1,0:T(8,128)(2,1)S(1)}, bf16[640,256]{1,0:T(8,128)(2,1)S(1)}, u32[]{:S(2)}, u32[]{:S(2)}) %collective-permute-start.3) | collective-permute-done | bytes 327712 | tf_op jit(solution)/shard_map/ppermute | solution.py:283
  53.3 2.1 %collective-permute-start.20 = (bf16[32,2048]{1,0:T(8,128)(2,1)S(1)}, bf16[32,2048]{1,0:T(8,128)(2,1)S(1)}, u32[]{:S(2)}, u32[]{:S(2)}) collective-permute-start(bf16[32,2048]{1,0:T(8,128)(2,1)S(1)} %get-tuple-element.94), channel_id=1, source_target_pairs={{0,6},{1,7},{2,4},{3,5},{4,2},{5,3},{6,0},{7,1},{8,14},{9,15},{10,... | collective-permute-start | bytes 393224 | tf_op jit(solution)/shard_map/ppermute | solution.py:283
  55.5 1.4 %product.2 = (f32[192,1920]{1,0:T(8,128)S(1)}, bf16[192,1920]{1,0:T(8,128)(2,1)S(1)}) custom-call(bf16[192,512]{1,0:T(8,128)(2,1)S(1)} %copy-done.1, bf16[192,512]{1,0:T(8,128)(2,1)S(1)} %collective-permute-done.1.kg_b, bf16[640,256]{1,0:T(8,128)(2,1)S(1)} %get-tuple-element.74.refs_0_, bf16[640,256]{1,0:T(8,128)(2,1)S(1)} %get-tuple-element.75.refs_1_, ...), custom_call_target="tpu_custom_call" | custom-call | tf_op jit(solution)/shard_map/product/pallas_call | solution.py:351
  56.9 1.0 %collective-permute-done.16 = bf16[32,2304]{1,0:T(8,128)(2,1)S(1)} collective-permute-done((bf16[32,2304]{1,0:T(8,128)(2,1)S(1)}, bf16[32,2304]{1,0:T(8,128)(2,1)S(1)}, u32[]{:S(2)}, u32[]{:S(2)}) %collective-permute-start.16) | collective-permute-done | bytes 147488 | tf_op jit(solution)/shard_map/ppermute | solution.py:283
  57.9 0.6 product.3
  59.1 2.1 %collective-permute-done.18 = bf16[32,2048]{1,0:T(8,128)(2,1)S(1)} collective-permute-done((bf16[32,2048]{1,0:T(8,128)(2,1)S(1)}, bf16[32,2048]{1,0:T(8,128)(2,1)S(1)}, u32[]{:S(2)}, u32[]{:S(2)}) %collective-permute-start.18) | collective-permute-done | bytes 131104 | tf_op jit(solution)/shard_map/ppermute | solution.py:283
  61.2 0.9 %pad_maximum_fusion = f32[32,5120]{1,0:T(8,128)} fusion(f32[32,2048]{1,0:T(8,128)S(1)} %fusion.3, f32[32,2304]{1,0:T(8,128)S(1)} %fusion, f32[32,768]{1,0:T(8,128)S(1)} %fusion.6), kind=kLoop, calls=%fused_computation.2 | loop fusion | flops 327680 | bytes 1310720 | tf_op jit(solution)/shard_map/concatenate | solution.py:427
  62.1 3.2 %token_grad.1 = bf16[192,5120]{1,0:T(8,128)(2,1)} custom-call(bf16[192,5120]{1,0:T(8,128)(2,1)S(1)} %copy-done, bf16[40,128]{1,0:T(8,128)(2,1)S(1)} %bitcast.5, f32[192,128]{1,0:T(8,128)S(1)} %get-tuple-element.49.inv_a.inv_ref, f32[192,1920]{1,0:T(8,128)S(1)} %get-tuple-element.90.refs_0_, bf16[192,1920]{1,0:T(8,128)(2,1)S(1)} %collective-permute-done.14.refs_1_, ...), custom_call_target="tpu_custom_call" | custom-call | tf_op jit(solution)/shard_map/token_grad/pallas_call | solution.py:413
  (39 shorter events, 3.3 us)
Async XLA Ops:
  0.6 9.1 %collective-permute-start.1 = (bf16[192,512]{1,0:T(8,128)(2,1)}, bf16[192,512]{1,0:T(8,128)(2,1)S(1)}, u32[]{:S(2)}, u32[]{:S(2)}) collective-permute-start(bf16[192,512]{1,0:T(8,128)(2,1)} %kg_a.3), channel_id=1, source_target_pairs={{0,1},{1,0},{2,3},{3,2},{4,5},{5,4},{6,7},{7,6},{8,9},{9,8},{10,11... | collective-permute-start | bytes 589832 | tf_op jit(solution)/shard_map/ppermute | solution.py:283
  1.1 8.6 %collective-permute-start = (bf16[192,5120]{1,0:T(8,128)(2,1)}, bf16[192,5120]{1,0:T(8,128)(2,1)S(1)}, u32[]{:S(2)}, u32[]{:S(2)}) collective-permute-start(bf16[192,5120]{1,0:T(8,128)(2,1)} %tok_hbm.7), channel_id=1, source_target_pairs={{0,1},{1,0},{2,3},{3,2},{4,5},{5,4},{6,7},{7,6},{8,9},{9,8},{10,11... | collective-permute-start | bytes 5898248 | tf_op jit(solution)/shard_map/ppermute | solution.py:283
  1.2 1.1 %copy-start.3 = (bf16[640,512]{1,0:T(8,128)(2,1)S(1)}, bf16[640,512]{1,0:T(8,128)(2,1)}, u32[]{:S(2)}) copy-start(bf16[640,512]{1,0:T(8,128)(2,1)} %code_hbm.1) | copy-start | bytes 1966084
  2.3 0.7 %copy-start.4 = (bf16[640,4]{0,1:T(4,128)(2,1)S(1)}, bf16[640,4]{0,1:T(4,128)(2,1)}, u32[]{:S(2)}) copy-start(bf16[640,4]{0,1:T(4,128)(2,1)} %param.9) | copy-start | bytes 15364
  3.0 6.7 %copy-start = (bf16[192,5120]{1,0:T(8,128)(2,1)S(1)}, bf16[192,5120]{1,0:T(8,128)(2,1)}, u32[]{:S(2)}) copy-start(bf16[192,5120]{1,0:T(8,128)(2,1)} %tok_hbm.7) | copy-start | bytes 5898244
  3.0 6.7 %copy-start.1 = (bf16[192,512]{1,0:T(8,128)(2,1)S(1)}, bf16[192,512]{1,0:T(8,128)(2,1)}, u32[]{:S(2)}) copy-start(bf16[192,512]{1,0:T(8,128)(2,1)} %kg_a.3) | copy-start | bytes 589828
  3.0 6.7 %copy-start.2 = (bf16[5120]{0:T(1024)(128)(2,1)S(1)}, bf16[5120]{0:T(1024)(128)(2,1)}, u32[]{:S(2)}) copy-start(bf16[5120]{0:T(1024)(128)(2,1)} %param.7) | copy-start | bytes 30724
  4.0 17.9 %collective-permute-start.2 = (bf16[640,256]{1,0:T(8,128)(2,1)S(1)}, bf16[640,256]{1,0:T(8,128)(2,1)S(1)}, u32[]{:S(2)}, u32[]{:S(2)}) collective-permute-start(bf16[640,256]{1,0:T(8,128)(2,1)S(1)} %get-tuple-element.74.refs_0_), channel_id=1, source_target_pairs={{0,2},{1,3},{2,0},{3,1},{4,6},{5,7},{6,4},{7,5},{8,10},{9,11},{10,... | collective-permute-start | bytes 983048 | tf_op jit(solution)/shard_map/ppermute | solution.py:283
  7.1 17.4 %collective-permute-start.4 = (bf16[640,256]{1,0:T(8,128)(2,1)S(1)}, bf16[640,256]{1,0:T(8,128)(2,1)S(1)}, u32[]{:S(2)}, u32[]{:S(2)}) collective-permute-start(bf16[640,256]{1,0:T(8,128)(2,1)S(1)} %get-tuple-element.74.refs_0_), channel_id=1, source_target_pairs={{0,4},{1,5},{2,6},{3,7},{4,0},{5,1},{6,2},{7,3},{8,12},{9,13},{10,... | collective-permute-start | bytes 983048 | tf_op jit(solution)/shard_map/ppermute | solution.py:283
  12.7 12.3 %collective-permute-start.7 = (bf16[128,768]{1,0:T(8,128)(2,1)S(1)}, bf16[128,768]{1,0:T(8,128)(2,1)S(1)}, u32[]{:S(2)}, u32[]{:S(2)}) collective-permute-start(bf16[128,768]{1,0:T(8,128)(2,1)S(1)} %get-tuple-element.61), channel_id=1, source_target_pairs={{0,8},{8,0},{1,9},{9,1},{2,10},{10,2},{3,11},{11,3},{4,12},{12,4},... | collective-permute-start | bytes 589832 | tf_op jit(solution)/shard_map/ppermute | solution.py:283
  15.9 16.1 %collective-permute-start.11 = (bf16[128,2304]{1,0:T(8,128)(2,1)S(1)}, bf16[128,2304]{1,0:T(8,128)(2,1)S(1)}, u32[]{:S(2)}, u32[]{:S(2)}) collective-permute-start(bf16[128,2304]{1,0:T(8,128)(2,1)S(1)} %get-tuple-element.64), channel_id=1, source_target_pairs={{0,8},{8,0},{1,9},{9,1},{2,10},{10,2},{3,11},{11,3},{4,12},{12,4},... | collective-permute-start | bytes 1769480 | tf_op jit(solution)/shard_map/ppermute | solution.py:283
  24.5 7.5 %collective-permute-start.12 = (bf16[640,256]{1,0:T(8,128)(2,1)S(1)}, bf16[640,256]{1,0:T(8,128)(2,1)S(1)}, u32[]{:S(2)}, u32[]{:S(2)}) collective-permute-start(bf16[640,256]{1,0:T(8,128)(2,1)S(1)} %collective-permute-done.4.refs_4_), channel_id=1, source_target_pairs={{0,2},{1,3},{2,0},{3,1},{4,6},{5,7},{6,4},{7,5},{8,10},{9,11},{10,... | collective-permute-start | bytes 983048 | tf_op jit(solution)/shard_map/ppermute | solution.py:283
  32.2 9.0 %collective-permute-start.13 = (bf16[64,2304]{1,0:T(8,128)(2,1)S(1)}, bf16[64,2304]{1,0:T(8,128)(2,1)S(1)}, u32[]{:S(2)}, u32[]{:S(2)}) collective-permute-start(bf16[64,2304]{1,0:T(8,128)(2,1)S(1)} %slice.88), channel_id=1, source_target_pairs={{0,2},{1,3},{2,0},{3,1},{4,6},{5,7},{6,4},{7,5},{8,10},{9,11},{10,... | collective-permute-start | bytes 884744 | tf_op jit(solution)/shard_map/ppermute | solution.py:283
  34.0 14.1 %collective-permute-start.6 = (bf16[128,2048]{1,0:T(8,128)(2,1)S(1)}, bf16[128,2048]{1,0:T(8,128)(2,1)S(1)}, u32[]{:S(2)}, u32[]{:S(2)}) collective-permute-start(bf16[128,2048]{1,0:T(8,128)(2,1)S(1)} %get-tuple-element.57), channel_id=1, source_target_pairs={{0,8},{8,0},{1,9},{9,1},{2,10},{10,2},{3,11},{11,3},{4,12},{12,4},... | collective-permute-start | bytes 1572872 | tf_op jit(solution)/shard_map/ppermute | solution.py:283
  35.5 13.5 %collective-permute-start.5 = (bf16[640,256]{1,0:T(8,128)(2,1)S(1)}, bf16[640,256]{1,0:T(8,128)(2,1)S(1)}, u32[]{:S(2)}, u32[]{:S(2)}) collective-permute-start(bf16[640,256]{1,0:T(8,128)(2,1)S(1)} %collective-permute-done.4.refs_4_), channel_id=1, source_target_pairs={{0,16},{16,0},{1,17},{17,1},{2,18},{18,2},{3,19},{19,3},{4,20},{20... | collective-permute-start | bytes 983048 | tf_op jit(solution)/shard_map/ppermute | solution.py:283
  37.0 6.4 %collective-permute-start.10 = (bf16[32,768]{1,0:T(8,128)(2,1)S(1)}, bf16[32,768]{1,0:T(8,128)(2,1)S(1)}, u32[]{:S(2)}, u32[]{:S(2)}) collective-permute-start(bf16[32,768]{1,0:T(8,128)(2,1)S(1)} %get-tuple-element.99), channel_id=1, source_target_pairs={{0,6},{1,7},{2,4},{3,5},{4,2},{5,3},{6,0},{7,1},{8,14},{9,15},{10,... | collective-permute-start | bytes 147464 | tf_op jit(solution)/shard_map/ppermute | solution.py:283
  39.1 5.9 %collective-permute-start.8 = (bf16[32,768]{1,0:T(8,128)(2,1)S(1)}, bf16[32,768]{1,0:T(8,128)(2,1)S(1)}, u32[]{:S(2)}, u32[]{:S(2)}) collective-permute-start(bf16[32,768]{1,0:T(8,128)(2,1)S(1)} %get-tuple-element.101), channel_id=1, source_target_pairs={{0,4},{1,5},{2,6},{3,7},{4,0},{5,1},{6,2},{7,3},{8,12},{9,13},{10,... | collective-permute-start | bytes 147464 | tf_op jit(solution)/shard_map/ppermute | solution.py:283
  41.2 4.6 %collective-permute-start.9 = (bf16[32,768]{1,0:T(8,128)(2,1)S(1)}, bf16[32,768]{1,0:T(8,128)(2,1)S(1)}, u32[]{:S(2)}, u32[]{:S(2)}) collective-permute-start(bf16[32,768]{1,0:T(8,128)(2,1)S(1)} %get-tuple-element.100), channel_id=1, source_target_pairs={{0,2},{1,3},{2,0},{3,1},{4,6},{5,7},{6,4},{7,5},{8,10},{9,11},{10,... | collective-permute-start | bytes 147464 | tf_op jit(solution)/shard_map/ppermute | solution.py:283
  43.4 9.9 %collective-permute-start.3 = (bf16[640,256]{1,0:T(8,128)(2,1)S(1)}, bf16[640,256]{1,0:T(8,128)(2,1)S(1)}, u32[]{:S(2)}, u32[]{:S(2)}) collective-permute-start(bf16[640,256]{1,0:T(8,128)(2,1)S(1)} %collective-permute-done.2.refs_2_), channel_id=1, source_target_pairs={{0,16},{16,0},{1,17},{17,1},{2,18},{18,2},{3,19},{19,3},{4,20},{20... | collective-permute-start | bytes 983048 | tf_op jit(solution)/shard_map/ppermute | solution.py:283
  45.0 12.9 %collective-permute-start.15 = (bf16[640,256]{1,0:T(8,128)(2,1)S(1)}, bf16[640,256]{1,0:T(8,128)(2,1)S(1)}, u32[]{:S(2)}, u32[]{:S(2)}) collective-permute-start(bf16[640,256]{1,0:T(8,128)(2,1)S(1)} %collective-permute-done.12.refs_0_), channel_id=1, source_target_pairs={{0,16},{16,0},{1,17},{17,1},{2,18},{18,2},{3,19},{19,3},{4,20},{20... | collective-permute-start | bytes 983048 | tf_op jit(solution)/shard_map/ppermute | solution.py:283
  45.8 12.1 %collective-permute-start.16 = (bf16[32,2304]{1,0:T(8,128)(2,1)S(1)}, bf16[32,2304]{1,0:T(8,128)(2,1)S(1)}, u32[]{:S(2)}, u32[]{:S(2)}) collective-permute-start(bf16[32,2304]{1,0:T(8,128)(2,1)S(1)} %slice.89), channel_id=1, source_target_pairs={{0,4},{1,5},{2,6},{3,7},{4,0},{5,1},{6,2},{7,3},{8,12},{9,13},{10,... | collective-permute-start | bytes 442376 | tf_op jit(solution)/shard_map/ppermute | solution.py:283
  48.3 12.9 %collective-permute-start.18 = (bf16[32,2048]{1,0:T(8,128)(2,1)S(1)}, bf16[32,2048]{1,0:T(8,128)(2,1)S(1)}, u32[]{:S(2)}, u32[]{:S(2)}) collective-permute-start(bf16[32,2048]{1,0:T(8,128)(2,1)S(1)} %get-tuple-element.96), channel_id=1, source_target_pairs={{0,4},{1,5},{2,6},{3,7},{4,0},{5,1},{6,2},{7,3},{8,12},{9,13},{10,... | collective-permute-start | bytes 393224 | tf_op jit(solution)/shard_map/ppermute | solution.py:283
  49.0 12.1 %collective-permute-start.19 = (bf16[32,2048]{1,0:T(8,128)(2,1)S(1)}, bf16[32,2048]{1,0:T(8,128)(2,1)S(1)}, u32[]{:S(2)}, u32[]{:S(2)}) collective-permute-start(bf16[32,2048]{1,0:T(8,128)(2,1)S(1)} %get-tuple-element.95), channel_id=1, source_target_pairs={{0,2},{1,3},{2,0},{3,1},{4,6},{5,7},{6,4},{7,5},{8,10},{9,11},{10,... | collective-permute-start | bytes 393224 | tf_op jit(solution)/shard_map/ppermute | solution.py:283
  53.3 7.8 %collective-permute-start.20 = (bf16[32,2048]{1,0:T(8,128)(2,1)S(1)}, bf16[32,2048]{1,0:T(8,128)(2,1)S(1)}, u32[]{:S(2)}, u32[]{:S(2)}) collective-permute-start(bf16[32,2048]{1,0:T(8,128)(2,1)S(1)} %get-tuple-element.94), channel_id=1, source_target_pairs={{0,6},{1,7},{2,4},{3,5},{4,2},{5,3},{6,0},{7,1},{8,14},{9,15},{10,... | collective-permute-start | bytes 393224 | tf_op jit(solution)/shard_map/ppermute | solution.py:283
  57.8 4.2 %collective-permute-start.14 = (bf16[192,1920]{1,0:T(8,128)(2,1)S(1)}, bf16[192,1920]{1,0:T(8,128)(2,1)S(1)}, u32[]{:S(2)}, u32[]{:S(2)}) collective-permute-start(bf16[192,1920]{1,0:T(8,128)(2,1)S(1)} %get-tuple-element.81), channel_id=1, source_target_pairs={{0,1},{1,0},{2,3},{3,2},{4,5},{5,4},{6,7},{7,6},{8,9},{9,8},{10,11... | collective-permute-start | bytes 2211848 | tf_op jit(solution)/shard_map/ppermute | solution.py:283
  58.5 3.6 %collective-permute-start.17 = (bf16[192,640]{1,0:T(8,128)(2,1)S(1)}, bf16[192,640]{1,0:T(8,128)(2,1)S(1)}, u32[]{:S(2)}, u32[]{:S(2)}) collective-permute-start(bf16[192,640]{1,0:T(8,128)(2,1)S(1)} %get-tuple-element.86), channel_id=1, source_target_pairs={{0,1},{1,0},{2,3},{3,2},{4,5},{5,4},{6,7},{7,6},{8,9},{9,8},{10,11... | collective-permute-start | bytes 737288 | tf_op jit(solution)/shard_map/ppermute | solution.py:283

commit v3 on v2

--- a/solution.py
+++ b/solution.py
@@ -14,12 +14,13 @@
 STAGES = 4
 COST_D = 20000000000.0
 COST_P = 0
+LATE = (-1, -1)
 COST_Q = 0
 COST_T = 0
 DIRECT = False
 CUTS = (768, 2304, 2048)
 GROUPS = ((2304,), (2048,))
-EVENTS = ('u1', 'u2', 'd0', 'u3', 'f1', 'g1', 'F0', 'd2', 'p', 'F1', 'q', 'F2', 't')
+EVENTS = ('u1', 'u2', 'f0', 'u3', 'g0', 'd1', 'F0', 'd2', 'p', 'F1', 'q', 'F2', 't')
 NT = (((1,), (1,)), ((), ()))
 
 
@@ -212,8 +213,15 @@
             out[:, n * width : (n + 1) * width] = value.astype(out.dtype)
 
 
-def token_kernel(counts, tok_hbm, gain_hbm, inv_ref, *refs):
-    pieces, (out_hbm, out_ref, scaled_ref, tok_ref, total_ref, gain_ref, gain, sems) = refs[:-8], refs[-8:]
+def token_kernel(counts, chunks, tok_hbm, gain_hbm, inv_ref, *refs):
+    owned, pieces = refs[:chunks], refs[chunks:-9]
+    out_hbm, weight_hbm, out_ref, scaled_ref, tok_ref, total_ref, gain_ref, gain, sems = refs[-9:]
+    copies, first = [], 0
+    for n, chunk in enumerate(owned):
+        target = weight_hbm.at[:, pl.ds(first, chunk.shape[1])]
+        copies.append(pltpu.make_async_copy(chunk, target, sems.at[2 + STAGES + n]))
+        copies[-1].start()
+        first += chunk.shape[1]
     arrived(fetch((gain_hbm, tok_hbm), (gain_ref, tok_ref), sems))
     rows, width = tok_ref.shape
     gain[...] = gain_ref[...].astype(F32)
@@ -259,7 +267,6 @@
         return carry
 
     stage = rows // STAGES
-    copies = []
     for n in range(STAGES):
         lax.fori_loop(n * stage // ROWS, (n + 1) * stage // ROWS, write, 0)
         r = pl.ds(n * stage, stage)
@@ -300,9 +307,6 @@
         ),
         n_in=2, far_in=(0, 1), flops=COST_D, name="decode",
     )(key_codes, code_scales.T)
-    units = {1: near(unit), 2: far(unit)}
-    if DIRECT:
-        units[3] = opposite(unit)
 
     gain_row = gain.reshape(width // 128, 128)
     cuts = CUTS
@@ -335,6 +339,9 @@
         first += total
     sent, kept = pairs[::2], pairs[1::2]
 
+    units = {k: move(after(unit, sent[n]) if n >= 0 else unit) for k, move, n in ((1, near, LATE[0]), (2, far, LATE[1]))}
+    if DIRECT:
+        units[3] = opposite(unit)
     got = [across(a) for a in sent]
     scale = 1 / math.sqrt(rows * lax.axis_size("wide") * lax.axis_size("narrow"))
     marker = [sent[-1]]
@@ -410,21 +417,19 @@
         elif kind == "F":
             finish(n)
         elif kind == "t":
-            token_grad = call(
-                functools.partial(token_kernel, (3, 1)),
-                S((rows, width), BF16),
+            token_grad, weight_grad = call(
+                functools.partial(token_kernel, (3, 1), len(cuts)),
+                (S((rows, width), BF16), S((32, width), F32)),
                 scratch=(
                     whole,
                     pltpu.VMEM((rows, width), F32),
                     whole,
                     pltpu.VMEM((rows, 128), F32),
                     *gains,
-                    pltpu.SemaphoreType.DMA((2 + STAGES,)),
+                    pltpu.SemaphoreType.DMA((2 + STAGES + len(cuts),)),
                 ),
-                n_in=7, far_in=(0, 1), far_out=True, flops=COST_T, name="token_grad",
-            )(tokens, gain_row, inv_a, *then((most, last))[0], *last)
-            mark(token_grad)
-    weight_grad = jnp.concatenate([owned[n] for n in range(len(cuts))], axis=1)
+                n_in=7 + len(cuts), far_in=(0, 1), far_out=True, flops=COST_T, name="token_grad",
+            )(tokens, gain_row, inv_a, *then([owned[n] for n in range(len(cuts))]), *most, *last)
     return (token_grad, weight_grad)
 
 

time: 65.5 us -> 65 us (level)
  other arithmetic: 1.39 us -> 0.52 us
    concatenate x1 -> x0, other arithmetic: 0.88 us -> none  [tuned(): weight_grad = jnp.concatenate([owned[n] for n in range(len(cuts))], axis=1)]
    ppermute x21, starting transfers between devices: 27.1 us -> 27.7 us  [tuned(): lax.ppermute(a, axis, swap_pairs(lax.axis_size(axis), bit))]
  transfers between devices with their start and end apart: 21 -> 21, of which waited for: 9 -> 6; matrix products, arithmetic and copies ran while one was open for 2% -> 1% of each run, Pallas kernels for 14% -> 14%
where the time goes in v3:
time: 65 us; the launch traced here: 64.9 us
  starting transfers between devices  27.7 us (43%)
  waiting for transfers between devices  21.5 us (33%)
  Pallas kernels  12.4 us (19%)
  local copies, waits for them, and re-layouts  1.87 us (3%)
  between operations  0.82 us (1%)
    ppermute x21, starting transfers between devices, tuned(): lax.ppermute(a, axis, swap_pairs(lax.axis_size(axis), bit))  27.7 us
    ppermute x21, waiting for transfers between devices, tuned(): lax.ppermute(a, axis, swap_pairs(lax.axis_size(axis), bit))  21.5 us
    pallas_call x2, Pallas kernels, tuned(): call(functools.partial(more_terms_kernel, first), tuple((S((128, cut), BF...  3.24 us
    pallas_call x1, Pallas kernels, tuned(): call(functools.partial(token_kernel, (3, 1), len(cuts)), (S((rows, width)...  3.23 us
    pallas_call x1, Pallas kernels, tuned(): call(first_term_kernel, (S((128, cuts[0]), BF16),) * 2 + (inv, inv, S((25...  2.95 us
    pallas_call x2, Pallas kernels, product(): call(functools.partial(product_kernel, n), (S((rows, n * shard), F32), S(...  1.98 us
    unnamed x10, local copies, waits for them, and re-layouts  1.79 us
  transfers between devices with their start and end apart: 21, of which 6 were waited for; matrix products, arithmetic and copies ran while one was open for 1% of the time, Pallas kernels for 14%

profile of v3, /device:TPU:0, one launch (start us, length us, event | category | flops | bytes accessed | tf_op | source)
XLA Modules:
  0.0 64.9 jit_solution(4915161961642290641)
XLA Ops:
  0.6 0.5 collective-permute-start
  1.2 1.1 %copy-done.3 = bf16[640,512]{1,0:T(8,128)(2,1)S(1)} copy-done((bf16[640,512]{1,0:T(8,128)(2,1)S(1)}, bf16[640,512]{1,0:T(8,128)(2,1)}, u32[]{:S(2)}) %copy-start.3) | copy-done | bytes 655384
  2.3 0.7 %copy-done.4 = bf16[640,4]{0,1:T(4,128)(2,1)S(1)} copy-done((bf16[640,4]{0,1:T(4,128)(2,1)S(1)}, bf16[640,4]{0,1:T(4,128)(2,1)}, u32[]{:S(2)}) %copy-start.4) | copy-done | bytes 5144
  3.0 1.0 %decode.1 = (bf16[640,256]{1,0:T(8,128)(2,1)S(1)}, bf16[640,256]{1,0:T(8,128)(2,1)S(1)}) custom-call(bf16[640,512]{1,0:T(8,128)(2,1)S(1)} %copy-done.3, bf16[4,640]{1,0:T(4,128)(2,1)S(1)} %bitcast.6), custom_call_target="tpu_custom_call" | custom-call | flops 20000000000 | tf_op jit(solution)/shard_map/decode/pallas_call | solution.py:300
  4.0 3.1 %collective-permute-start.4 = (bf16[640,256]{1,0:T(8,128)(2,1)S(1)}, bf16[640,256]{1,0:T(8,128)(2,1)S(1)}, u32[]{:S(2)}, u32[]{:S(2)}) collective-permute-start(bf16[640,256]{1,0:T(8,128)(2,1)S(1)} %get-tuple-element.73.refs_0_), channel_id=1, source_target_pairs={{0,2},{1,3},{2,0},{3,1},{4,6},{5,7},{6,4},{7,5},{8,10},{9,11},{10,... | collective-permute-start | bytes 983048 | tf_op jit(solution)/shard_map/ppermute | solution.py:290
  7.1 2.6 %collective-permute-start.3 = (bf16[640,256]{1,0:T(8,128)(2,1)S(1)}, bf16[640,256]{1,0:T(8,128)(2,1)S(1)}, u32[]{:S(2)}, u32[]{:S(2)}) collective-permute-start(bf16[640,256]{1,0:T(8,128)(2,1)S(1)} %get-tuple-element.73.refs_0_), channel_id=1, source_target_pairs={{0,4},{1,5},{2,6},{3,7},{4,0},{5,1},{6,2},{7,3},{8,12},{9,13},{10,... | collective-permute-start | bytes 983048 | tf_op jit(solution)/shard_map/ppermute | solution.py:290
  9.7 3.0 %first_term.1 = (bf16[128,768]{1,0:T(8,128)(2,1)S(1)}, bf16[128,768]{1,0:T(8,128)(2,1)S(1)}, f32[192,128]{1,0:T(8,128)S(1)}, f32[192,128]{1,0:T(8,128)S(1)}, bf16[256,384]{1,0:T(8,128)(2,1)S(1)}) custom-call(bf16[192,5120]{1,0:T(8,128)(2,1)S(1)} %copy-done, bf16[192,512]{1,0:T(8,128)(2,1)S(1)} %copy-done.1, bf16[40,128]{1,0:T(8,128)(2,1)S(1)} %bitcast.2, ...), custom_call_target="tpu_custom_call" | custom-call | tf_op jit(solution)/shard_map/first_term/pallas_call | solution.py:316
  12.7 1.6 %collective-permute-start.2 = (bf16[128,768]{1,0:T(8,128)(2,1)S(1)}, bf16[128,768]{1,0:T(8,128)(2,1)S(1)}, u32[]{:S(2)}, u32[]{:S(2)}) collective-permute-start(bf16[128,768]{1,0:T(8,128)(2,1)S(1)} %get-tuple-element.52), channel_id=1, source_target_pairs={{0,8},{8,0},{1,9},{9,1},{2,10},{10,2},{3,11},{11,3},{4,12},{12,4},... | collective-permute-start | bytes 589832 | tf_op jit(solution)/shard_map/ppermute | solution.py:290
  14.2 1.7 %more_terms.2 = (bf16[128,2304]{1,0:T(8,128)(2,1)S(1)}, bf16[128,2304]{1,0:T(8,128)(2,1)S(1)}) custom-call(bf16[192,5120]{1,0:T(8,128)(2,1)S(1)} %copy-done, bf16[40,128]{1,0:T(8,128)(2,1)S(1)} %bitcast.3, bf16[192,5120]{1,0:T(8,128)(2,1)S(1)} %collective-permute-done.tok_b, f32[192,128]{1,0:T(8,128)S(1)} %get-tuple-element.50.inv_a.inv_ref, ...), custom_call_target="tpu_custom_call" | custom-call | tf_op jit(solution)/shard_map/more_terms/pallas_call | solution.py:332
  15.9 0.6 collective-permute-start.8
  16.5 1.6 %more_terms.3 = (bf16[128,2048]{1,0:T(8,128)(2,1)S(1)}, bf16[128,2048]{1,0:T(8,128)(2,1)S(1)}) custom-call(bf16[192,5120]{1,0:T(8,128)(2,1)S(1)} %copy-done, bf16[40,128]{1,0:T(8,128)(2,1)S(1)} %bitcast.4, bf16[192,5120]{1,0:T(8,128)(2,1)S(1)} %collective-permute-done.tok_b, f32[192,128]{1,0:T(8,128)S(1)} %get-tuple-element.50.inv_a.inv_ref, ...), custom_call_target="tpu_custom_call" | custom-call | tf_op jit(solution)/shard_map/more_terms/pallas_call | solution.py:332
  18.1 3.9 %collective-permute-done.4.refs_2_ = bf16[640,256]{1,0:T(8,128)(2,1)S(1)} collective-permute-done((bf16[640,256]{1,0:T(8,128)(2,1)S(1)}, bf16[640,256]{1,0:T(8,128)(2,1)S(1)}, u32[]{:S(2)}, u32[]{:S(2)}) %collective-permute-start.4) | collective-permute-done | bytes 327712 | tf_op jit(solution)/shard_map/ppermute | solution.py:290
  22.0 2.5 %collective-permute-done.3.refs_4_ = bf16[640,256]{1,0:T(8,128)(2,1)S(1)} collective-permute-done((bf16[640,256]{1,0:T(8,128)(2,1)S(1)}, bf16[640,256]{1,0:T(8,128)(2,1)S(1)}, u32[]{:S(2)}, u32[]{:S(2)}) %collective-permute-start.3) | collective-permute-done | bytes 327712 | tf_op jit(solution)/shard_map/ppermute | solution.py:290
  24.5 0.4 collective-permute-start.6
  25.0 1.6 %collective-permute-start.5 = (bf16[64,768]{1,0:T(8,128)(2,1)S(1)}, bf16[64,768]{1,0:T(8,128)(2,1)S(1)}, u32[]{:S(2)}, u32[]{:S(2)}) collective-permute-start(bf16[64,768]{1,0:T(8,128)(2,1)S(1)} %slice.88), channel_id=1, source_target_pairs={{0,2},{1,3},{2,0},{3,1},{4,6},{5,7},{6,4},{7,5},{8,10},{9,11},{10,... | collective-permute-start | bytes 294920 | tf_op jit(solution)/shard_map/ppermute | solution.py:290
  26.6 1.5 %collective-permute-start.12 = (bf16[640,256]{1,0:T(8,128)(2,1)S(1)}, bf16[640,256]{1,0:T(8,128)(2,1)S(1)}, u32[]{:S(2)}, u32[]{:S(2)}) collective-permute-start(bf16[640,256]{1,0:T(8,128)(2,1)S(1)} %collective-permute-done.4.refs_2_), channel_id=1, source_target_pairs={{0,16},{16,0},{1,17},{17,1},{2,18},{18,2},{3,19},{19,3},{4,20},{20... | collective-permute-start | bytes 983048 | tf_op jit(solution)/shard_map/ppermute | solution.py:290
  28.2 0.5 collective-permute-start.13
  28.7 4.4 %collective-permute-done.6.refs_0_ = bf16[640,256]{1,0:T(8,128)(2,1)S(1)} collective-permute-done((bf16[640,256]{1,0:T(8,128)(2,1)S(1)}, bf16[640,256]{1,0:T(8,128)(2,1)S(1)}, u32[]{:S(2)}, u32[]{:S(2)}) %collective-permute-start.6) | collective-permute-done | bytes 327712 | tf_op jit(solution)/shard_map/ppermute | solution.py:290
  33.0 1.5 %collective-permute-start.14 = (bf16[128,2048]{1,0:T(8,128)(2,1)S(1)}, bf16[128,2048]{1,0:T(8,128)(2,1)S(1)}, u32[]{:S(2)}, u32[]{:S(2)}) collective-permute-start(bf16[128,2048]{1,0:T(8,128)(2,1)S(1)} %get-tuple-element.58), channel_id=1, source_target_pairs={{0,8},{8,0},{1,9},{9,1},{2,10},{10,2},{3,11},{11,3},{4,12},{12,4},... | collective-permute-start | bytes 1572872 | tf_op jit(solution)/shard_map/ppermute | solution.py:290
  34.6 2.4 %collective-permute-start.7 = (bf16[32,768]{1,0:T(8,128)(2,1)S(1)}, bf16[32,768]{1,0:T(8,128)(2,1)S(1)}, u32[]{:S(2)}, u32[]{:S(2)}) collective-permute-start(bf16[32,768]{1,0:T(8,128)(2,1)S(1)} %slice.89), channel_id=1, source_target_pairs={{0,4},{1,5},{2,6},{3,7},{4,0},{5,1},{6,2},{7,3},{8,12},{9,13},{10,... | collective-permute-start | bytes 147464 | tf_op jit(solution)/shard_map/ppermute | solution.py:290
  37.2 0.6 collective-permute-start.9
  37.8 4.5 %collective-permute-done.7 = bf16[32,768]{1,0:T(8,128)(2,1)S(1)} collective-permute-done((bf16[32,768]{1,0:T(8,128)(2,1)S(1)}, bf16[32,768]{1,0:T(8,128)(2,1)S(1)}, u32[]{:S(2)}, u32[]{:S(2)}) %collective-permute-start.7) | collective-permute-done | bytes 49184 | tf_op jit(solution)/shard_map/ppermute | solution.py:290
  42.4 1.0 %collective-permute-done.14 = bf16[128,2048]{1,0:T(8,128)(2,1)S(1)} collective-permute-done((bf16[128,2048]{1,0:T(8,128)(2,1)S(1)}, bf16[128,2048]{1,0:T(8,128)(2,1)S(1)}, u32[]{:S(2)}, u32[]{:S(2)}) %collective-permute-start.14) | collective-permute-done | bytes 524320 | tf_op jit(solution)/shard_map/ppermute | solution.py:290
  43.3 4.1 %collective-permute-start.11 = (bf16[32,2304]{1,0:T(8,128)(2,1)S(1)}, bf16[32,2304]{1,0:T(8,128)(2,1)S(1)}, u32[]{:S(2)}, u32[]{:S(2)}) collective-permute-start(bf16[32,2304]{1,0:T(8,128)(2,1)S(1)} %get-tuple-element.98), channel_id=1, source_target_pairs={{0,6},{1,7},{2,4},{3,5},{4,2},{5,3},{6,0},{7,1},{8,14},{9,15},{10,... | collective-permute-start | bytes 442376 | tf_op jit(solution)/shard_map/ppermute | solution.py:290
  47.6 1.6 %collective-permute-start.18 = (bf16[640,256]{1,0:T(8,128)(2,1)S(1)}, bf16[640,256]{1,0:T(8,128)(2,1)S(1)}, u32[]{:S(2)}, u32[]{:S(2)}) collective-permute-start(bf16[640,256]{1,0:T(8,128)(2,1)S(1)} %collective-permute-done.6.refs_0_), channel_id=1, source_target_pairs={{0,16},{16,0},{1,17},{17,1},{2,18},{18,2},{3,19},{19,3},{4,20},{20... | collective-permute-start | bytes 983048 | tf_op jit(solution)/shard_map/ppermute | solution.py:290
  49.2 1.4 %product.2 = (f32[192,1920]{1,0:T(8,128)S(1)}, bf16[192,1920]{1,0:T(8,128)(2,1)S(1)}) custom-call(bf16[192,512]{1,0:T(8,128)(2,1)S(1)} %copy-done.1, bf16[192,512]{1,0:T(8,128)(2,1)S(1)} %collective-permute-done.1.kg_b, bf16[640,256]{1,0:T(8,128)(2,1)S(1)} %get-tuple-element.73.refs_0_, bf16[640,256]{1,0:T(8,128)(2,1)S(1)} %get-tuple-element.74.refs_1_, ...), custom_call_target="tpu_custom_call" | custom-call | tf_op jit(solution)/shard_map/product/pallas_call | solution.py:358
  50.6 0.6 collective-permute-start.16
  51.3 3.8 %collective-permute-start.17 = (bf16[32,2048]{1,0:T(8,128)(2,1)S(1)}, bf16[32,2048]{1,0:T(8,128)(2,1)S(1)}, u32[]{:S(2)}, u32[]{:S(2)}) collective-permute-start(bf16[32,2048]{1,0:T(8,128)(2,1)S(1)} %get-tuple-element.101), channel_id=1, source_target_pairs={{0,6},{1,7},{2,4},{3,5},{4,2},{5,3},{6,0},{7,1},{8,14},{9,15},{10,... | collective-permute-start | bytes 393224 | tf_op jit(solution)/shard_map/ppermute | solution.py:290
  55.2 0.6 product.3
  55.8 0.6 collective-permute-start.20
  56.3 5.2 %collective-permute-done.15 = bf16[32,2048]{1,0:T(8,128)(2,1)S(1)} collective-permute-done((bf16[32,2048]{1,0:T(8,128)(2,1)S(1)}, bf16[32,2048]{1,0:T(8,128)(2,1)S(1)}, u32[]{:S(2)}, u32[]{:S(2)}) %collective-permute-start.15) | collective-permute-done | bytes 131104 | tf_op jit(solution)/shard_map/ppermute | solution.py:290
  61.6 3.2 %token_grad.1 = (bf16[192,5120]{1,0:T(8,128)(2,1)}, f32[32,5120]{1,0:T(8,128)}) custom-call(bf16[192,5120]{1,0:T(8,128)(2,1)S(1)} %copy-done, bf16[40,128]{1,0:T(8,128)(2,1)S(1)} %bitcast.5, f32[192,128]{1,0:T(8,128)S(1)} %get-tuple-element.50.inv_a.inv_ref, f32[32,768]{1,0:T(8,128)S(1)} %fusion.6.refs_0_, f32[32,2304]{1,0:T(8,128)S(1)} %fusion.2.refs_1_, ...), custom_call_target="tpu_custom_call" | custom-call | tf_op jit(solution)/shard_map/token_grad/pallas_call | solution.py:420
  (38 shorter events, 0.7 us)
Async XLA Ops:
  0.6 9.1 %collective-permute-start = (bf16[192,5120]{1,0:T(8,128)(2,1)}, bf16[192,5120]{1,0:T(8,128)(2,1)S(1)}, u32[]{:S(2)}, u32[]{:S(2)}) collective-permute-start(bf16[192,5120]{1,0:T(8,128)(2,1)} %tok_hbm.7), channel_id=1, source_target_pairs={{0,1},{1,0},{2,3},{3,2},{4,5},{5,4},{6,7},{7,6},{8,9},{9,8},{10,11... | collective-permute-start | bytes 5898248 | tf_op jit(solution)/shard_map/ppermute | solution.py:290
  1.1 8.5 %collective-permute-start.1 = (bf16[192,512]{1,0:T(8,128)(2,1)}, bf16[192,512]{1,0:T(8,128)(2,1)S(1)}, u32[]{:S(2)}, u32[]{:S(2)}) collective-permute-start(bf16[192,512]{1,0:T(8,128)(2,1)} %kg_a.3), channel_id=1, source_target_pairs={{0,1},{1,0},{2,3},{3,2},{4,5},{5,4},{6,7},{7,6},{8,9},{9,8},{10,11... | collective-permute-start | bytes 589832 | tf_op jit(solution)/shard_map/ppermute | solution.py:290
  1.2 1.1 %copy-start.3 = (bf16[640,512]{1,0:T(8,128)(2,1)S(1)}, bf16[640,512]{1,0:T(8,128)(2,1)}, u32[]{:S(2)}) copy-start(bf16[640,512]{1,0:T(8,128)(2,1)} %code_hbm.1) | copy-start | bytes 1966084
  2.3 0.7 %copy-start.4 = (bf16[640,4]{0,1:T(4,128)(2,1)S(1)}, bf16[640,4]{0,1:T(4,128)(2,1)}, u32[]{:S(2)}) copy-start(bf16[640,4]{0,1:T(4,128)(2,1)} %param.9) | copy-start | bytes 15364
  3.0 6.7 %copy-start = (bf16[192,5120]{1,0:T(8,128)(2,1)S(1)}, bf16[192,5120]{1,0:T(8,128)(2,1)}, u32[]{:S(2)}) copy-start(bf16[192,5120]{1,0:T(8,128)(2,1)} %tok_hbm.7) | copy-start | bytes 5898244
  3.0 6.7 %copy-start.1 = (bf16[192,512]{1,0:T(8,128)(2,1)S(1)}, bf16[192,512]{1,0:T(8,128)(2,1)}, u32[]{:S(2)}) copy-start(bf16[192,512]{1,0:T(8,128)(2,1)} %kg_a.3) | copy-start | bytes 589828
  3.0 6.7 %copy-start.2 = (bf16[5120]{0:T(1024)(128)(2,1)S(1)}, bf16[5120]{0:T(1024)(128)(2,1)}, u32[]{:S(2)}) copy-start(bf16[5120]{0:T(1024)(128)(2,1)} %param.7) | copy-start | bytes 30724
  4.0 17.9 %collective-permute-start.4 = (bf16[640,256]{1,0:T(8,128)(2,1)S(1)}, bf16[640,256]{1,0:T(8,128)(2,1)S(1)}, u32[]{:S(2)}, u32[]{:S(2)}) collective-permute-start(bf16[640,256]{1,0:T(8,128)(2,1)S(1)} %get-tuple-element.73.refs_0_), channel_id=1, source_target_pairs={{0,2},{1,3},{2,0},{3,1},{4,6},{5,7},{6,4},{7,5},{8,10},{9,11},{10,... | collective-permute-start | bytes 983048 | tf_op jit(solution)/shard_map/ppermute | solution.py:290
  7.1 17.4 %collective-permute-start.3 = (bf16[640,256]{1,0:T(8,128)(2,1)S(1)}, bf16[640,256]{1,0:T(8,128)(2,1)S(1)}, u32[]{:S(2)}, u32[]{:S(2)}) collective-permute-start(bf16[640,256]{1,0:T(8,128)(2,1)S(1)} %get-tuple-element.73.refs_0_), channel_id=1, source_target_pairs={{0,4},{1,5},{2,6},{3,7},{4,0},{5,1},{6,2},{7,3},{8,12},{9,13},{10,... | collective-permute-start | bytes 983048 | tf_op jit(solution)/shard_map/ppermute | solution.py:290
  12.7 12.3 %collective-permute-start.2 = (bf16[128,768]{1,0:T(8,128)(2,1)S(1)}, bf16[128,768]{1,0:T(8,128)(2,1)S(1)}, u32[]{:S(2)}, u32[]{:S(2)}) collective-permute-start(bf16[128,768]{1,0:T(8,128)(2,1)S(1)} %get-tuple-element.52), channel_id=1, source_target_pairs={{0,8},{8,0},{1,9},{9,1},{2,10},{10,2},{3,11},{11,3},{4,12},{12,4},... | collective-permute-start | bytes 589832 | tf_op jit(solution)/shard_map/ppermute | solution.py:290
  15.9 21.1 %collective-permute-start.8 = (bf16[128,2304]{1,0:T(8,128)(2,1)S(1)}, bf16[128,2304]{1,0:T(8,128)(2,1)S(1)}, u32[]{:S(2)}, u32[]{:S(2)}) collective-permute-start(bf16[128,2304]{1,0:T(8,128)(2,1)S(1)} %get-tuple-element.65), channel_id=1, source_target_pairs={{0,8},{8,0},{1,9},{9,1},{2,10},{10,2},{3,11},{11,3},{4,12},{12,4},... | collective-permute-start | bytes 1769480 | tf_op jit(solution)/shard_map/ppermute | solution.py:290
  24.5 8.6 %collective-permute-start.6 = (bf16[640,256]{1,0:T(8,128)(2,1)S(1)}, bf16[640,256]{1,0:T(8,128)(2,1)S(1)}, u32[]{:S(2)}, u32[]{:S(2)}) collective-permute-start(bf16[640,256]{1,0:T(8,128)(2,1)S(1)} %collective-permute-done.3.refs_4_), channel_id=1, source_target_pairs={{0,2},{1,3},{2,0},{3,1},{4,6},{5,7},{6,4},{7,5},{8,10},{9,11},{10,... | collective-permute-start | bytes 983048 | tf_op jit(solution)/shard_map/ppermute | solution.py:290
  25.0 9.5 %collective-permute-start.5 = (bf16[64,768]{1,0:T(8,128)(2,1)S(1)}, bf16[64,768]{1,0:T(8,128)(2,1)S(1)}, u32[]{:S(2)}, u32[]{:S(2)}) collective-permute-start(bf16[64,768]{1,0:T(8,128)(2,1)S(1)} %slice.88), channel_id=1, source_target_pairs={{0,2},{1,3},{2,0},{3,1},{4,6},{5,7},{6,4},{7,5},{8,10},{9,11},{10,... | collective-permute-start | bytes 294920 | tf_op jit(solution)/shard_map/ppermute | solution.py:290
  26.6 21.0 %collective-permute-start.12 = (bf16[640,256]{1,0:T(8,128)(2,1)S(1)}, bf16[640,256]{1,0:T(8,128)(2,1)S(1)}, u32[]{:S(2)}, u32[]{:S(2)}) collective-permute-start(bf16[640,256]{1,0:T(8,128)(2,1)S(1)} %collective-permute-done.4.refs_2_), channel_id=1, source_target_pairs={{0,16},{16,0},{1,17},{17,1},{2,18},{18,2},{3,19},{19,3},{4,20},{20... | collective-permute-start | bytes 983048 | tf_op jit(solution)/shard_map/ppermute | solution.py:290
  28.2 21.0 %collective-permute-start.13 = (bf16[640,256]{1,0:T(8,128)(2,1)S(1)}, bf16[640,256]{1,0:T(8,128)(2,1)S(1)}, u32[]{:S(2)}, u32[]{:S(2)}) collective-permute-start(bf16[640,256]{1,0:T(8,128)(2,1)S(1)} %collective-permute-done.3.refs_4_), channel_id=1, source_target_pairs={{0,16},{16,0},{1,17},{17,1},{2,18},{18,2},{3,19},{19,3},{4,20},{20... | collective-permute-start | bytes 983048 | tf_op jit(solution)/shard_map/ppermute | solution.py:290
  33.0 10.3 %collective-permute-start.14 = (bf16[128,2048]{1,0:T(8,128)(2,1)S(1)}, bf16[128,2048]{1,0:T(8,128)(2,1)S(1)}, u32[]{:S(2)}, u32[]{:S(2)}) collective-permute-start(bf16[128,2048]{1,0:T(8,128)(2,1)S(1)} %get-tuple-element.58), channel_id=1, source_target_pairs={{0,8},{8,0},{1,9},{9,1},{2,10},{10,2},{3,11},{11,3},{4,12},{12,4},... | collective-permute-start | bytes 1572872 | tf_op jit(solution)/shard_map/ppermute | solution.py:290
  34.6 7.7 %collective-permute-start.7 = (bf16[32,768]{1,0:T(8,128)(2,1)S(1)}, bf16[32,768]{1,0:T(8,128)(2,1)S(1)}, u32[]{:S(2)}, u32[]{:S(2)}) collective-permute-start(bf16[32,768]{1,0:T(8,128)(2,1)S(1)} %slice.89), channel_id=1, source_target_pairs={{0,4},{1,5},{2,6},{3,7},{4,0},{5,1},{6,2},{7,3},{8,12},{9,13},{10,... | collective-permute-start | bytes 147464 | tf_op jit(solution)/shard_map/ppermute | solution.py:290
  37.2 13.4 %collective-permute-start.9 = (bf16[32,2304]{1,0:T(8,128)(2,1)S(1)}, bf16[32,2304]{1,0:T(8,128)(2,1)S(1)}, u32[]{:S(2)}, u32[]{:S(2)}) collective-permute-start(bf16[32,2304]{1,0:T(8,128)(2,1)S(1)} %get-tuple-element.100), channel_id=1, source_target_pairs={{0,4},{1,5},{2,6},{3,7},{4,0},{5,1},{6,2},{7,3},{8,12},{9,13},{10,... | collective-permute-start | bytes 442376 | tf_op jit(solution)/shard_map/ppermute | solution.py:290
  42.3 8.9 %collective-permute-start.10 = (bf16[32,2304]{1,0:T(8,128)(2,1)S(1)}, bf16[32,2304]{1,0:T(8,128)(2,1)S(1)}, u32[]{:S(2)}, u32[]{:S(2)}) collective-permute-start(bf16[32,2304]{1,0:T(8,128)(2,1)S(1)} %get-tuple-element.99), channel_id=1, source_target_pairs={{0,2},{1,3},{2,0},{3,1},{4,6},{5,7},{6,4},{7,5},{8,10},{9,11},{10,... | collective-permute-start | bytes 442376 | tf_op jit(solution)/shard_map/ppermute | solution.py:290
  43.3 11.7 %collective-permute-start.11 = (bf16[32,2304]{1,0:T(8,128)(2,1)S(1)}, bf16[32,2304]{1,0:T(8,128)(2,1)S(1)}, u32[]{:S(2)}, u32[]{:S(2)}) collective-permute-start(bf16[32,2304]{1,0:T(8,128)(2,1)S(1)} %get-tuple-element.98), channel_id=1, source_target_pairs={{0,6},{1,7},{2,4},{3,5},{4,2},{5,3},{6,0},{7,1},{8,14},{9,15},{10,... | collective-permute-start | bytes 442376 | tf_op jit(solution)/shard_map/ppermute | solution.py:290
  47.6 7.6 %collective-permute-start.18 = (bf16[640,256]{1,0:T(8,128)(2,1)S(1)}, bf16[640,256]{1,0:T(8,128)(2,1)S(1)}, u32[]{:S(2)}, u32[]{:S(2)}) collective-permute-start(bf16[640,256]{1,0:T(8,128)(2,1)S(1)} %collective-permute-done.6.refs_0_), channel_id=1, source_target_pairs={{0,16},{16,0},{1,17},{17,1},{2,18},{18,2},{3,19},{19,3},{4,20},{20... | collective-permute-start | bytes 983048 | tf_op jit(solution)/shard_map/ppermute | solution.py:290
  49.2 12.3 %collective-permute-start.15 = (bf16[32,2048]{1,0:T(8,128)(2,1)S(1)}, bf16[32,2048]{1,0:T(8,128)(2,1)S(1)}, u32[]{:S(2)}, u32[]{:S(2)}) collective-permute-start(bf16[32,2048]{1,0:T(8,128)(2,1)S(1)} %get-tuple-element.103), channel_id=1, source_target_pairs={{0,4},{1,5},{2,6},{3,7},{4,0},{5,1},{6,2},{7,3},{8,12},{9,13},{10,... | collective-permute-start | bytes 393224 | tf_op jit(solution)/shard_map/ppermute | solution.py:290
  50.6 10.9 %collective-permute-start.16 = (bf16[32,2048]{1,0:T(8,128)(2,1)S(1)}, bf16[32,2048]{1,0:T(8,128)(2,1)S(1)}, u32[]{:S(2)}, u32[]{:S(2)}) collective-permute-start(bf16[32,2048]{1,0:T(8,128)(2,1)S(1)} %get-tuple-element.102), channel_id=1, source_target_pairs={{0,2},{1,3},{2,0},{3,1},{4,6},{5,7},{6,4},{7,5},{8,10},{9,11},{10,... | collective-permute-start | bytes 393224 | tf_op jit(solution)/shard_map/ppermute | solution.py:290
  51.3 10.3 %collective-permute-start.17 = (bf16[32,2048]{1,0:T(8,128)(2,1)S(1)}, bf16[32,2048]{1,0:T(8,128)(2,1)S(1)}, u32[]{:S(2)}, u32[]{:S(2)}) collective-permute-start(bf16[32,2048]{1,0:T(8,128)(2,1)S(1)} %get-tuple-element.101), channel_id=1, source_target_pairs={{0,6},{1,7},{2,4},{3,5},{4,2},{5,3},{6,0},{7,1},{8,14},{9,15},{10,... | collective-permute-start | bytes 393224 | tf_op jit(solution)/shard_map/ppermute | solution.py:290
  55.1 6.5 %collective-permute-start.19 = (bf16[192,1920]{1,0:T(8,128)(2,1)S(1)}, bf16[192,1920]{1,0:T(8,128)(2,1)S(1)}, u32[]{:S(2)}, u32[]{:S(2)}) collective-permute-start(bf16[192,1920]{1,0:T(8,128)(2,1)S(1)} %get-tuple-element.79), channel_id=1, source_target_pairs={{0,1},{1,0},{2,3},{3,2},{4,5},{5,4},{6,7},{7,6},{8,9},{9,8},{10,11... | collective-permute-start | bytes 2211848 | tf_op jit(solution)/shard_map/ppermute | solution.py:290
  55.8 5.8 %collective-permute-start.20 = (bf16[192,640]{1,0:T(8,128)(2,1)S(1)}, bf16[192,640]{1,0:T(8,128)(2,1)S(1)}, u32[]{:S(2)}, u32[]{:S(2)}) collective-permute-start(bf16[192,640]{1,0:T(8,128)(2,1)S(1)} %get-tuple-element.85), channel_id=1, source_target_pairs={{0,1},{1,0},{2,3},{3,2},{4,5},{5,4},{6,7},{7,6},{8,9},{9,8},{10,11... | collective-permute-start | bytes 737288 | tf_op jit(solution)/shard_map/ppermute | solution.py:290

commit v4 on v3

--- a/solution.py
+++ b/solution.py
@@ -101,7 +101,7 @@
         inv_ref[r, :] = (totals[0] + totals[1]) + (totals[2] + totals[3])
         return carry
 
-    lax.fori_loop(0, rows // ROWS, step, 0)
+    lax.fori_loop(0, rows // ROWS, step, 0, unroll=2)
     mean = jnp.sum(inv_ref[...], axis=1, keepdims=True) * (1.0 / width)
     inv_ref[...] = jnp.broadcast_to(lax.rsqrt(mean + EPS), inv_ref.shape)
 
@@ -151,7 +151,7 @@
             normed[pl.ds(base + at, ROWS), j : j + 128] = (v * scale * g).astype(BF16)
         return carry
 
-    lax.fori_loop(0, tok.shape[0] // ROWS, step, 0)
+    lax.fori_loop(0, tok.shape[0] // ROWS, step, 0, unroll=2)
 
 
 def term_into(picked, normed, sent_ref, kept_ref, first):
@@ -250,7 +250,7 @@
         total_ref[r, :] = ((totals[0] + totals[1]) + (totals[2] + totals[3])) * inv_ref[r, :]
         return carry
 
-    lax.fori_loop(0, rows // ROWS, weigh, 0)
+    lax.fori_loop(0, rows // ROWS, weigh, 0, unroll=2)
     mean = jnp.sum(total_ref[...], axis=1, keepdims=True) * (1.0 / width)
     total_ref[...] = jnp.broadcast_to(mean, total_ref.shape)
 
@@ -268,7 +268,7 @@
 
     stage = rows // STAGES
     for n in range(STAGES):
-        lax.fori_loop(n * stage // ROWS, (n + 1) * stage // ROWS, write, 0)
+        lax.fori_loop(n * stage // ROWS, (n + 1) * stage // ROWS, write, 0, unroll=3)
         r = pl.ds(n * stage, stage)
         copies.append(pltpu.make_async_copy(out_ref.at[r], out_hbm.at[r], sems.at[2 + n]))
         copies[-1].start()

time: 65 us -> 64.8 us (level)
  no operation moved by 1% of the time
where the time goes in v4:
time: 64.8 us; the launch traced here: 64.6 us
  starting transfers between devices  27.7 us (43%)
  waiting for transfers between devices  21.6 us (33%)
  Pallas kernels  12.1 us (19%)
  local copies, waits for them, and re-layouts  1.87 us (3%)
  between operations  0.82 us (1%)
    ppermute x21, starting transfers between devices, tuned(): lax.ppermute(a, axis, swap_pairs(lax.axis_size(axis), bit))  27.7 us
    ppermute x21, waiting for transfers between devices, tuned(): lax.ppermute(a, axis, swap_pairs(lax.axis_size(axis), bit))  21.6 us
    pallas_call x2, Pallas kernels, tuned(): call(functools.partial(more_terms_kernel, first), tuple((S((128, cut), BF...  3.26 us
    pallas_call x1, Pallas kernels, tuned(): call(functools.partial(token_kernel, (3, 1), len(cuts)), (S((rows, width)...  3.02 us
    pallas_call x1, Pallas kernels, tuned(): call(first_term_kernel, (S((128, cuts[0]), BF16),) * 2 + (inv, inv, S((25...  2.82 us
    pallas_call x2, Pallas kernels, product(): call(functools.partial(product_kernel, n), (S((rows, n * shard), F32), S(...  1.98 us
    unnamed x10, local copies, waits for them, and re-layouts  1.79 us
  transfers between devices with their start and end apart: 21, of which 6 were waited for; matrix products, arithmetic and copies ran while one was open for 1% of the time, Pallas kernels for 14%

profile of v4, /device:TPU:0, one launch (start us, length us, event | category | flops | bytes accessed | tf_op | source)
XLA Modules:
  0.0 64.6 jit_solution(10892124583333276118)
XLA Ops:
  0.6 0.5 collective-permute-start
  1.2 1.1 %copy-done.3 = bf16[640,512]{1,0:T(8,128)(2,1)S(1)} copy-done((bf16[640,512]{1,0:T(8,128)(2,1)S(1)}, bf16[640,512]{1,0:T(8,128)(2,1)}, u32[]{:S(2)}) %copy-start.3) | copy-done | bytes 655384
  2.3 0.7 %copy-done.4 = bf16[640,4]{0,1:T(4,128)(2,1)S(1)} copy-done((bf16[640,4]{0,1:T(4,128)(2,1)S(1)}, bf16[640,4]{0,1:T(4,128)(2,1)}, u32[]{:S(2)}) %copy-start.4) | copy-done | bytes 5144
  3.0 1.0 %decode.1 = (bf16[640,256]{1,0:T(8,128)(2,1)S(1)}, bf16[640,256]{1,0:T(8,128)(2,1)S(1)}) custom-call(bf16[640,512]{1,0:T(8,128)(2,1)S(1)} %copy-done.3, bf16[4,640]{1,0:T(4,128)(2,1)S(1)} %bitcast.6), custom_call_target="tpu_custom_call" | custom-call | flops 20000000000 | tf_op jit(solution)/shard_map/decode/pallas_call | solution.py:300
  4.0 3.1 %collective-permute-start.4 = (bf16[640,256]{1,0:T(8,128)(2,1)S(1)}, bf16[640,256]{1,0:T(8,128)(2,1)S(1)}, u32[]{:S(2)}, u32[]{:S(2)}) collective-permute-start(bf16[640,256]{1,0:T(8,128)(2,1)S(1)} %get-tuple-element.73.refs_0_), channel_id=1, source_target_pairs={{0,2},{1,3},{2,0},{3,1},{4,6},{5,7},{6,4},{7,5},{8,10},{9,11},{10,... | collective-permute-start | bytes 983048 | tf_op jit(solution)/shard_map/ppermute | solution.py:290
  7.1 2.6 %collective-permute-start.3 = (bf16[640,256]{1,0:T(8,128)(2,1)S(1)}, bf16[640,256]{1,0:T(8,128)(2,1)S(1)}, u32[]{:S(2)}, u32[]{:S(2)}) collective-permute-start(bf16[640,256]{1,0:T(8,128)(2,1)S(1)} %get-tuple-element.73.refs_0_), channel_id=1, source_target_pairs={{0,4},{1,5},{2,6},{3,7},{4,0},{5,1},{6,2},{7,3},{8,12},{9,13},{10,... | collective-permute-start | bytes 983048 | tf_op jit(solution)/shard_map/ppermute | solution.py:290
  9.7 2.8 %first_term.1 = (bf16[128,768]{1,0:T(8,128)(2,1)S(1)}, bf16[128,768]{1,0:T(8,128)(2,1)S(1)}, f32[192,128]{1,0:T(8,128)S(1)}, f32[192,128]{1,0:T(8,128)S(1)}, bf16[256,384]{1,0:T(8,128)(2,1)S(1)}) custom-call(bf16[192,5120]{1,0:T(8,128)(2,1)S(1)} %copy-done, bf16[192,512]{1,0:T(8,128)(2,1)S(1)} %copy-done.1, bf16[40,128]{1,0:T(8,128)(2,1)S(1)} %bitcast.2, ...), custom_call_target="tpu_custom_call" | custom-call | tf_op jit(solution)/shard_map/first_term/pallas_call | solution.py:316
  12.6 1.5 %collective-permute-start.2 = (bf16[128,768]{1,0:T(8,128)(2,1)S(1)}, bf16[128,768]{1,0:T(8,128)(2,1)S(1)}, u32[]{:S(2)}, u32[]{:S(2)}) collective-permute-start(bf16[128,768]{1,0:T(8,128)(2,1)S(1)} %get-tuple-element.52), channel_id=1, source_target_pairs={{0,8},{8,0},{1,9},{9,1},{2,10},{10,2},{3,11},{11,3},{4,12},{12,4},... | collective-permute-start | bytes 589832 | tf_op jit(solution)/shard_map/ppermute | solution.py:290
  14.1 1.7 %more_terms.2 = (bf16[128,2304]{1,0:T(8,128)(2,1)S(1)}, bf16[128,2304]{1,0:T(8,128)(2,1)S(1)}) custom-call(bf16[192,5120]{1,0:T(8,128)(2,1)S(1)} %copy-done, bf16[40,128]{1,0:T(8,128)(2,1)S(1)} %bitcast.3, bf16[192,5120]{1,0:T(8,128)(2,1)S(1)} %collective-permute-done.tok_b, f32[192,128]{1,0:T(8,128)S(1)} %get-tuple-element.50.inv_a.inv_ref, ...), custom_call_target="tpu_custom_call" | custom-call | tf_op jit(solution)/shard_map/more_terms/pallas_call | solution.py:332
  15.8 0.6 collective-permute-start.8
  16.4 1.6 %more_terms.3 = (bf16[128,2048]{1,0:T(8,128)(2,1)S(1)}, bf16[128,2048]{1,0:T(8,128)(2,1)S(1)}) custom-call(bf16[192,5120]{1,0:T(8,128)(2,1)S(1)} %copy-done, bf16[40,128]{1,0:T(8,128)(2,1)S(1)} %bitcast.4, bf16[192,5120]{1,0:T(8,128)(2,1)S(1)} %collective-permute-done.tok_b, f32[192,128]{1,0:T(8,128)S(1)} %get-tuple-element.50.inv_a.inv_ref, ...), custom_call_target="tpu_custom_call" | custom-call | tf_op jit(solution)/shard_map/more_terms/pallas_call | solution.py:332
  18.0 4.0 %collective-permute-done.4.refs_2_ = bf16[640,256]{1,0:T(8,128)(2,1)S(1)} collective-permute-done((bf16[640,256]{1,0:T(8,128)(2,1)S(1)}, bf16[640,256]{1,0:T(8,128)(2,1)S(1)}, u32[]{:S(2)}, u32[]{:S(2)}) %collective-permute-start.4) | collective-permute-done | bytes 327712 | tf_op jit(solution)/shard_map/ppermute | solution.py:290
  22.0 2.5 %collective-permute-done.3.refs_4_ = bf16[640,256]{1,0:T(8,128)(2,1)S(1)} collective-permute-done((bf16[640,256]{1,0:T(8,128)(2,1)S(1)}, bf16[640,256]{1,0:T(8,128)(2,1)S(1)}, u32[]{:S(2)}, u32[]{:S(2)}) %collective-permute-start.3) | collective-permute-done | bytes 327712 | tf_op jit(solution)/shard_map/ppermute | solution.py:290
  24.5 0.4 collective-permute-start.6
  25.0 1.6 %collective-permute-start.5 = (bf16[64,768]{1,0:T(8,128)(2,1)S(1)}, bf16[64,768]{1,0:T(8,128)(2,1)S(1)}, u32[]{:S(2)}, u32[]{:S(2)}) collective-permute-start(bf16[64,768]{1,0:T(8,128)(2,1)S(1)} %slice.88), channel_id=1, source_target_pairs={{0,2},{1,3},{2,0},{3,1},{4,6},{5,7},{6,4},{7,5},{8,10},{9,11},{10,... | collective-permute-start | bytes 294920 | tf_op jit(solution)/shard_map/ppermute | solution.py:290
  26.6 1.5 %collective-permute-start.12 = (bf16[640,256]{1,0:T(8,128)(2,1)S(1)}, bf16[640,256]{1,0:T(8,128)(2,1)S(1)}, u32[]{:S(2)}, u32[]{:S(2)}) collective-permute-start(bf16[640,256]{1,0:T(8,128)(2,1)S(1)} %collective-permute-done.4.refs_2_), channel_id=1, source_target_pairs={{0,16},{16,0},{1,17},{17,1},{2,18},{18,2},{3,19},{19,3},{4,20},{20... | collective-permute-start | bytes 983048 | tf_op jit(solution)/shard_map/ppermute | solution.py:290
  28.2 0.5 collective-permute-start.13
  28.7 4.4 %collective-permute-done.6.refs_0_ = bf16[640,256]{1,0:T(8,128)(2,1)S(1)} collective-permute-done((bf16[640,256]{1,0:T(8,128)(2,1)S(1)}, bf16[640,256]{1,0:T(8,128)(2,1)S(1)}, u32[]{:S(2)}, u32[]{:S(2)}) %collective-permute-start.6) | collective-permute-done | bytes 327712 | tf_op jit(solution)/shard_map/ppermute | solution.py:290
  33.0 1.5 %collective-permute-start.14 = (bf16[128,2048]{1,0:T(8,128)(2,1)S(1)}, bf16[128,2048]{1,0:T(8,128)(2,1)S(1)}, u32[]{:S(2)}, u32[]{:S(2)}) collective-permute-start(bf16[128,2048]{1,0:T(8,128)(2,1)S(1)} %get-tuple-element.58), channel_id=1, source_target_pairs={{0,8},{8,0},{1,9},{9,1},{2,10},{10,2},{3,11},{11,3},{4,12},{12,4},... | collective-permute-start | bytes 1572872 | tf_op jit(solution)/shard_map/ppermute | solution.py:290
  34.6 2.4 %collective-permute-start.7 = (bf16[32,768]{1,0:T(8,128)(2,1)S(1)}, bf16[32,768]{1,0:T(8,128)(2,1)S(1)}, u32[]{:S(2)}, u32[]{:S(2)}) collective-permute-start(bf16[32,768]{1,0:T(8,128)(2,1)S(1)} %slice.89), channel_id=1, source_target_pairs={{0,4},{1,5},{2,6},{3,7},{4,0},{5,1},{6,2},{7,3},{8,12},{9,13},{10,... | collective-permute-start | bytes 147464 | tf_op jit(solution)/shard_map/ppermute | solution.py:290
  37.2 0.6 collective-permute-start.9
  37.8 4.5 %collective-permute-done.7 = bf16[32,768]{1,0:T(8,128)(2,1)S(1)} collective-permute-done((bf16[32,768]{1,0:T(8,128)(2,1)S(1)}, bf16[32,768]{1,0:T(8,128)(2,1)S(1)}, u32[]{:S(2)}, u32[]{:S(2)}) %collective-permute-start.7) | collective-permute-done | bytes 49184 | tf_op jit(solution)/shard_map/ppermute | solution.py:290
  42.4 1.0 %collective-permute-done.14 = bf16[128,2048]{1,0:T(8,128)(2,1)S(1)} collective-permute-done((bf16[128,2048]{1,0:T(8,128)(2,1)S(1)}, bf16[128,2048]{1,0:T(8,128)(2,1)S(1)}, u32[]{:S(2)}, u32[]{:S(2)}) %collective-permute-start.14) | collective-permute-done | bytes 524320 | tf_op jit(solution)/shard_map/ppermute | solution.py:290
  43.3 4.1 %collective-permute-start.11 = (bf16[32,2304]{1,0:T(8,128)(2,1)S(1)}, bf16[32,2304]{1,0:T(8,128)(2,1)S(1)}, u32[]{:S(2)}, u32[]{:S(2)}) collective-permute-start(bf16[32,2304]{1,0:T(8,128)(2,1)S(1)} %get-tuple-element.98), channel_id=1, source_target_pairs={{0,6},{1,7},{2,4},{3,5},{4,2},{5,3},{6,0},{7,1},{8,14},{9,15},{10,... | collective-permute-start | bytes 442376 | tf_op jit(solution)/shard_map/ppermute | solution.py:290
  47.6 1.6 %collective-permute-start.18 = (bf16[640,256]{1,0:T(8,128)(2,1)S(1)}, bf16[640,256]{1,0:T(8,128)(2,1)S(1)}, u32[]{:S(2)}, u32[]{:S(2)}) collective-permute-start(bf16[640,256]{1,0:T(8,128)(2,1)S(1)} %collective-permute-done.6.refs_0_), channel_id=1, source_target_pairs={{0,16},{16,0},{1,17},{17,1},{2,18},{18,2},{3,19},{19,3},{4,20},{20... | collective-permute-start | bytes 983048 | tf_op jit(solution)/shard_map/ppermute | solution.py:290
  49.2 1.4 %product.2 = (f32[192,1920]{1,0:T(8,128)S(1)}, bf16[192,1920]{1,0:T(8,128)(2,1)S(1)}) custom-call(bf16[192,512]{1,0:T(8,128)(2,1)S(1)} %copy-done.1, bf16[192,512]{1,0:T(8,128)(2,1)S(1)} %collective-permute-done.1.kg_b, bf16[640,256]{1,0:T(8,128)(2,1)S(1)} %get-tuple-element.73.refs_0_, bf16[640,256]{1,0:T(8,128)(2,1)S(1)} %get-tuple-element.74.refs_1_, ...), custom_call_target="tpu_custom_call" | custom-call | tf_op jit(solution)/shard_map/product/pallas_call | solution.py:358
  50.6 0.6 collective-permute-start.16
  51.3 3.8 %collective-permute-start.17 = (bf16[32,2048]{1,0:T(8,128)(2,1)S(1)}, bf16[32,2048]{1,0:T(8,128)(2,1)S(1)}, u32[]{:S(2)}, u32[]{:S(2)}) collective-permute-start(bf16[32,2048]{1,0:T(8,128)(2,1)S(1)} %get-tuple-element.101), channel_id=1, source_target_pairs={{0,6},{1,7},{2,4},{3,5},{4,2},{5,3},{6,0},{7,1},{8,14},{9,15},{10,... | collective-permute-start | bytes 393224 | tf_op jit(solution)/shard_map/ppermute | solution.py:290
  55.2 0.6 product.3
  55.8 0.6 collective-permute-start.20
  56.3 5.2 %collective-permute-done.15 = bf16[32,2048]{1,0:T(8,128)(2,1)S(1)} collective-permute-done((bf16[32,2048]{1,0:T(8,128)(2,1)S(1)}, bf16[32,2048]{1,0:T(8,128)(2,1)S(1)}, u32[]{:S(2)}, u32[]{:S(2)}) %collective-permute-start.15) | collective-permute-done | bytes 131104 | tf_op jit(solution)/shard_map/ppermute | solution.py:290
  61.6 3.0 %token_grad.1 = (bf16[192,5120]{1,0:T(8,128)(2,1)}, f32[32,5120]{1,0:T(8,128)}) custom-call(bf16[192,5120]{1,0:T(8,128)(2,1)S(1)} %copy-done, bf16[40,128]{1,0:T(8,128)(2,1)S(1)} %bitcast.5, f32[192,128]{1,0:T(8,128)S(1)} %get-tuple-element.50.inv_a.inv_ref, f32[32,768]{1,0:T(8,128)S(1)} %fusion.6.refs_0_, f32[32,2304]{1,0:T(8,128)S(1)} %fusion.2.refs_1_, ...), custom_call_target="tpu_custom_call" | custom-call | tf_op jit(solution)/shard_map/token_grad/pallas_call | solution.py:420
  (38 shorter events, 0.7 us)
Async XLA Ops:
  0.6 9.1 %collective-permute-start = (bf16[192,5120]{1,0:T(8,128)(2,1)}, bf16[192,5120]{1,0:T(8,128)(2,1)S(1)}, u32[]{:S(2)}, u32[]{:S(2)}) collective-permute-start(bf16[192,5120]{1,0:T(8,128)(2,1)} %tok_hbm.7), channel_id=1, source_target_pairs={{0,1},{1,0},{2,3},{3,2},{4,5},{5,4},{6,7},{7,6},{8,9},{9,8},{10,11... | collective-permute-start | bytes 5898248 | tf_op jit(solution)/shard_map/ppermute | solution.py:290
  1.1 8.5 %collective-permute-start.1 = (bf16[192,512]{1,0:T(8,128)(2,1)}, bf16[192,512]{1,0:T(8,128)(2,1)S(1)}, u32[]{:S(2)}, u32[]{:S(2)}) collective-permute-start(bf16[192,512]{1,0:T(8,128)(2,1)} %kg_a.3), channel_id=1, source_target_pairs={{0,1},{1,0},{2,3},{3,2},{4,5},{5,4},{6,7},{7,6},{8,9},{9,8},{10,11... | collective-permute-start | bytes 589832 | tf_op jit(solution)/shard_map/ppermute | solution.py:290
  1.2 1.1 %copy-start.3 = (bf16[640,512]{1,0:T(8,128)(2,1)S(1)}, bf16[640,512]{1,0:T(8,128)(2,1)}, u32[]{:S(2)}) copy-start(bf16[640,512]{1,0:T(8,128)(2,1)} %code_hbm.1) | copy-start | bytes 1966084
  2.3 0.7 %copy-start.4 = (bf16[640,4]{0,1:T(4,128)(2,1)S(1)}, bf16[640,4]{0,1:T(4,128)(2,1)}, u32[]{:S(2)}) copy-start(bf16[640,4]{0,1:T(4,128)(2,1)} %param.9) | copy-start | bytes 15364
  3.0 6.7 %copy-start = (bf16[192,5120]{1,0:T(8,128)(2,1)S(1)}, bf16[192,5120]{1,0:T(8,128)(2,1)}, u32[]{:S(2)}) copy-start(bf16[192,5120]{1,0:T(8,128)(2,1)} %tok_hbm.7) | copy-start | bytes 5898244
  3.0 6.7 %copy-start.1 = (bf16[192,512]{1,0:T(8,128)(2,1)S(1)}, bf16[192,512]{1,0:T(8,128)(2,1)}, u32[]{:S(2)}) copy-start(bf16[192,512]{1,0:T(8,128)(2,1)} %kg_a.3) | copy-start | bytes 589828
  3.0 6.7 %copy-start.2 = (bf16[5120]{0:T(1024)(128)(2,1)S(1)}, bf16[5120]{0:T(1024)(128)(2,1)}, u32[]{:S(2)}) copy-start(bf16[5120]{0:T(1024)(128)(2,1)} %param.7) | copy-start | bytes 30724
  4.0 17.9 %collective-permute-start.4 = (bf16[640,256]{1,0:T(8,128)(2,1)S(1)}, bf16[640,256]{1,0:T(8,128)(2,1)S(1)}, u32[]{:S(2)}, u32[]{:S(2)}) collective-permute-start(bf16[640,256]{1,0:T(8,128)(2,1)S(1)} %get-tuple-element.73.refs_0_), channel_id=1, source_target_pairs={{0,2},{1,3},{2,0},{3,1},{4,6},{5,7},{6,4},{7,5},{8,10},{9,11},{10,... | collective-permute-start | bytes 983048 | tf_op jit(solution)/shard_map/ppermute | solution.py:290
  7.1 17.4 %collective-permute-start.3 = (bf16[640,256]{1,0:T(8,128)(2,1)S(1)}, bf16[640,256]{1,0:T(8,128)(2,1)S(1)}, u32[]{:S(2)}, u32[]{:S(2)}) collective-permute-start(bf16[640,256]{1,0:T(8,128)(2,1)S(1)} %get-tuple-element.73.refs_0_), channel_id=1, source_target_pairs={{0,4},{1,5},{2,6},{3,7},{4,0},{5,1},{6,2},{7,3},{8,12},{9,13},{10,... | collective-permute-start | bytes 983048 | tf_op jit(solution)/shard_map/ppermute | solution.py:290
  12.6 12.4 %collective-permute-start.2 = (bf16[128,768]{1,0:T(8,128)(2,1)S(1)}, bf16[128,768]{1,0:T(8,128)(2,1)S(1)}, u32[]{:S(2)}, u32[]{:S(2)}) collective-permute-start(bf16[128,768]{1,0:T(8,128)(2,1)S(1)} %get-tuple-element.52), channel_id=1, source_target_pairs={{0,8},{8,0},{1,9},{9,1},{2,10},{10,2},{3,11},{11,3},{4,12},{12,4},... | collective-permute-start | bytes 589832 | tf_op jit(solution)/shard_map/ppermute | solution.py:290
  15.8 21.2 %collective-permute-start.8 = (bf16[128,2304]{1,0:T(8,128)(2,1)S(1)}, bf16[128,2304]{1,0:T(8,128)(2,1)S(1)}, u32[]{:S(2)}, u32[]{:S(2)}) collective-permute-start(bf16[128,2304]{1,0:T(8,128)(2,1)S(1)} %get-tuple-element.65), channel_id=1, source_target_pairs={{0,8},{8,0},{1,9},{9,1},{2,10},{10,2},{3,11},{11,3},{4,12},{12,4},... | collective-permute-start | bytes 1769480 | tf_op jit(solution)/shard_map/ppermute | solution.py:290
  24.5 8.6 %collective-permute-start.6 = (bf16[640,256]{1,0:T(8,128)(2,1)S(1)}, bf16[640,256]{1,0:T(8,128)(2,1)S(1)}, u32[]{:S(2)}, u32[]{:S(2)}) collective-permute-start(bf16[640,256]{1,0:T(8,128)(2,1)S(1)} %collective-permute-done.3.refs_4_), channel_id=1, source_target_pairs={{0,2},{1,3},{2,0},{3,1},{4,6},{5,7},{6,4},{7,5},{8,10},{9,11},{10,... | collective-permute-start | bytes 983048 | tf_op jit(solution)/shard_map/ppermute | solution.py:290
  25.0 9.5 %collective-permute-start.5 = (bf16[64,768]{1,0:T(8,128)(2,1)S(1)}, bf16[64,768]{1,0:T(8,128)(2,1)S(1)}, u32[]{:S(2)}, u32[]{:S(2)}) collective-permute-start(bf16[64,768]{1,0:T(8,128)(2,1)S(1)} %slice.88), channel_id=1, source_target_pairs={{0,2},{1,3},{2,0},{3,1},{4,6},{5,7},{6,4},{7,5},{8,10},{9,11},{10,... | collective-permute-start | bytes 294920 | tf_op jit(solution)/shard_map/ppermute | solution.py:290
  26.6 21.0 %collective-permute-start.12 = (bf16[640,256]{1,0:T(8,128)(2,1)S(1)}, bf16[640,256]{1,0:T(8,128)(2,1)S(1)}, u32[]{:S(2)}, u32[]{:S(2)}) collective-permute-start(bf16[640,256]{1,0:T(8,128)(2,1)S(1)} %collective-permute-done.4.refs_2_), channel_id=1, source_target_pairs={{0,16},{16,0},{1,17},{17,1},{2,18},{18,2},{3,19},{19,3},{4,20},{20... | collective-permute-start | bytes 983048 | tf_op jit(solution)/shard_map/ppermute | solution.py:290
  28.2 21.0 %collective-permute-start.13 = (bf16[640,256]{1,0:T(8,128)(2,1)S(1)}, bf16[640,256]{1,0:T(8,128)(2,1)S(1)}, u32[]{:S(2)}, u32[]{:S(2)}) collective-permute-start(bf16[640,256]{1,0:T(8,128)(2,1)S(1)} %collective-permute-done.3.refs_4_), channel_id=1, source_target_pairs={{0,16},{16,0},{1,17},{17,1},{2,18},{18,2},{3,19},{19,3},{4,20},{20... | collective-permute-start | bytes 983048 | tf_op jit(solution)/shard_map/ppermute | solution.py:290
  33.0 10.3 %collective-permute-start.14 = (bf16[128,2048]{1,0:T(8,128)(2,1)S(1)}, bf16[128,2048]{1,0:T(8,128)(2,1)S(1)}, u32[]{:S(2)}, u32[]{:S(2)}) collective-permute-start(bf16[128,2048]{1,0:T(8,128)(2,1)S(1)} %get-tuple-element.58), channel_id=1, source_target_pairs={{0,8},{8,0},{1,9},{9,1},{2,10},{10,2},{3,11},{11,3},{4,12},{12,4},... | collective-permute-start | bytes 1572872 | tf_op jit(solution)/shard_map/ppermute | solution.py:290
  34.6 7.7 %collective-permute-start.7 = (bf16[32,768]{1,0:T(8,128)(2,1)S(1)}, bf16[32,768]{1,0:T(8,128)(2,1)S(1)}, u32[]{:S(2)}, u32[]{:S(2)}) collective-permute-start(bf16[32,768]{1,0:T(8,128)(2,1)S(1)} %slice.89), channel_id=1, source_target_pairs={{0,4},{1,5},{2,6},{3,7},{4,0},{5,1},{6,2},{7,3},{8,12},{9,13},{10,... | collective-permute-start | bytes 147464 | tf_op jit(solution)/shard_map/ppermute | solution.py:290
  37.2 13.4 %collective-permute-start.9 = (bf16[32,2304]{1,0:T(8,128)(2,1)S(1)}, bf16[32,2304]{1,0:T(8,128)(2,1)S(1)}, u32[]{:S(2)}, u32[]{:S(2)}) collective-permute-start(bf16[32,2304]{1,0:T(8,128)(2,1)S(1)} %get-tuple-element.100), channel_id=1, source_target_pairs={{0,4},{1,5},{2,6},{3,7},{4,0},{5,1},{6,2},{7,3},{8,12},{9,13},{10,... | collective-permute-start | bytes 442376 | tf_op jit(solution)/shard_map/ppermute | solution.py:290
  42.3 8.9 %collective-permute-start.10 = (bf16[32,2304]{1,0:T(8,128)(2,1)S(1)}, bf16[32,2304]{1,0:T(8,128)(2,1)S(1)}, u32[]{:S(2)}, u32[]{:S(2)}) collective-permute-start(bf16[32,2304]{1,0:T(8,128)(2,1)S(1)} %get-tuple-element.99), channel_id=1, source_target_pairs={{0,2},{1,3},{2,0},{3,1},{4,6},{5,7},{6,4},{7,5},{8,10},{9,11},{10,... | collective-permute-start | bytes 442376 | tf_op jit(solution)/shard_map/ppermute | solution.py:290
  43.3 11.7 %collective-permute-start.11 = (bf16[32,2304]{1,0:T(8,128)(2,1)S(1)}, bf16[32,2304]{1,0:T(8,128)(2,1)S(1)}, u32[]{:S(2)}, u32[]{:S(2)}) collective-permute-start(bf16[32,2304]{1,0:T(8,128)(2,1)S(1)} %get-tuple-element.98), channel_id=1, source_target_pairs={{0,6},{1,7},{2,4},{3,5},{4,2},{5,3},{6,0},{7,1},{8,14},{9,15},{10,... | collective-permute-start | bytes 442376 | tf_op jit(solution)/shard_map/ppermute | solution.py:290
  47.6 7.6 %collective-permute-start.18 = (bf16[640,256]{1,0:T(8,128)(2,1)S(1)}, bf16[640,256]{1,0:T(8,128)(2,1)S(1)}, u32[]{:S(2)}, u32[]{:S(2)}) collective-permute-start(bf16[640,256]{1,0:T(8,128)(2,1)S(1)} %collective-permute-done.6.refs_0_), channel_id=1, source_target_pairs={{0,16},{16,0},{1,17},{17,1},{2,18},{18,2},{3,19},{19,3},{4,20},{20... | collective-permute-start | bytes 983048 | tf_op jit(solution)/shard_map/ppermute | solution.py:290
  49.2 12.3 %collective-permute-start.15 = (bf16[32,2048]{1,0:T(8,128)(2,1)S(1)}, bf16[32,2048]{1,0:T(8,128)(2,1)S(1)}, u32[]{:S(2)}, u32[]{:S(2)}) collective-permute-start(bf16[32,2048]{1,0:T(8,128)(2,1)S(1)} %get-tuple-element.103), channel_id=1, source_target_pairs={{0,4},{1,5},{2,6},{3,7},{4,0},{5,1},{6,2},{7,3},{8,12},{9,13},{10,... | collective-permute-start | bytes 393224 | tf_op jit(solution)/shard_map/ppermute | solution.py:290
  50.6 10.9 %collective-permute-start.16 = (bf16[32,2048]{1,0:T(8,128)(2,1)S(1)}, bf16[32,2048]{1,0:T(8,128)(2,1)S(1)}, u32[]{:S(2)}, u32[]{:S(2)}) collective-permute-start(bf16[32,2048]{1,0:T(8,128)(2,1)S(1)} %get-tuple-element.102), channel_id=1, source_target_pairs={{0,2},{1,3},{2,0},{3,1},{4,6},{5,7},{6,4},{7,5},{8,10},{9,11},{10,... | collective-permute-start | bytes 393224 | tf_op jit(solution)/shard_map/ppermute | solution.py:290
  51.3 10.3 %collective-permute-start.17 = (bf16[32,2048]{1,0:T(8,128)(2,1)S(1)}, bf16[32,2048]{1,0:T(8,128)(2,1)S(1)}, u32[]{:S(2)}, u32[]{:S(2)}) collective-permute-start(bf16[32,2048]{1,0:T(8,128)(2,1)S(1)} %get-tuple-element.101), channel_id=1, source_target_pairs={{0,6},{1,7},{2,4},{3,5},{4,2},{5,3},{6,0},{7,1},{8,14},{9,15},{10,... | collective-permute-start | bytes 393224 | tf_op jit(solution)/shard_map/ppermute | solution.py:290
  55.1 6.5 %collective-permute-start.19 = (bf16[192,1920]{1,0:T(8,128)(2,1)S(1)}, bf16[192,1920]{1,0:T(8,128)(2,1)S(1)}, u32[]{:S(2)}, u32[]{:S(2)}) collective-permute-start(bf16[192,1920]{1,0:T(8,128)(2,1)S(1)} %get-tuple-element.79), channel_id=1, source_target_pairs={{0,1},{1,0},{2,3},{3,2},{4,5},{5,4},{6,7},{7,6},{8,9},{9,8},{10,11... | collective-permute-start | bytes 2211848 | tf_op jit(solution)/shard_map/ppermute | solution.py:290
  55.8 5.8 %collective-permute-start.20 = (bf16[192,640]{1,0:T(8,128)(2,1)S(1)}, bf16[192,640]{1,0:T(8,128)(2,1)S(1)}, u32[]{:S(2)}, u32[]{:S(2)}) collective-permute-start(bf16[192,640]{1,0:T(8,128)(2,1)S(1)} %get-tuple-element.85), channel_id=1, source_target_pairs={{0,1},{1,0},{2,3},{3,2},{4,5},{5,4},{6,7},{7,6},{8,9},{9,8},{10,11... | collective-permute-start | bytes 737288 | tf_op jit(solution)/shard_map/ppermute | solution.py:290
